TPU v7x, 128 devices: a whole 4x4x4 slice. The times are simulated.
128 devices in a mesh: depth: 8 (over x_hi, y), yband: 16 (over x_lo, z, core).
Axes of the slice: x: 4 (x_hi: 2, x_lo: 2; x = x_hi * 2 + x_lo), y: 4, z: 4, core: 2. Of those that a mesh axis runs over, the one named last changes fastest.
Arguments:
- projections: bfloat16 [16, 256, 2048], P('depth', 'yband'), may hold values from -16 to 16
- angle_index: int32 [16], replicated, may hold values from 0 to 1439
- row_ranges: int32 [16, 2], P('yband'), may hold values from -12 to 268, as said below
Outputs:
- banded: float32 [128, 128, 1024], P(('depth', 'yband'))
Inputs may be any that keep to these rules, and one draw needn't show every extreme that they name: `row_ranges`: band b accepts rows from b * 16 - 12 + r to (b + 1) * 16 + 12 - q, with r and q from 0 to 11; r is 0 for the first band and q is 0 for the last.
All inputs are finite; a program needn't handle non-finite values.
Results may differ from a plain program's by a relative error of at most 0.0095.
Values may be sent and summed in bfloat16 or wider, within the bound.
A program may use at most 128 MiB of HBM per device.

v0:
```python
import math

import jax
import jax.numpy as jnp
from jax import lax
from jax.sharding import PartitionSpec as P

NX = 1024
NU = 2048
NANG = 1440
NP_DEV = 2
YB_DEV = 8
ZS_DEV = 16
RB_DEV = 16
HALO = 12


lower_edge = 0.04
upper_edge = 0.35
highest = lax.Precision.HIGHEST


def padded(cells, sides, width):
    for axis, dim in sides:
        count = lax.axis_size(axis)
        ends = count - 1
        head = lax.slice_in_dim(cells, 0, width, axis=dim)
        tail = lax.slice_in_dim(cells, cells.shape[dim] - width, cells.shape[dim], axis=dim)
        cells = jnp.concatenate(
            [
                lax.ppermute(tail, axis, [(i, (i + 1) % count) for i in range(ends)]),
                cells,
                lax.ppermute(head, axis, [((i + 1) % count, i) for i in range(ends)]),
            ],
            axis=dim,
        )
    return cells


def ramp_table():
    offset = jnp.arange(NU, dtype=jnp.int32)[:, None] - jnp.arange(NU, dtype=jnp.int32)[None, :]
    odd_offset = offset % 2 == 1
    distance = jnp.where(odd_offset, offset, 1).astype(jnp.float32)
    spacing = NX / NU
    values = jnp.where(
        offset == 0,
        0.25,
        jnp.where(odd_offset, -1.0 / (math.pi * math.pi * distance * distance), 0.0),
    )
    return (values / spacing).astype(jnp.bfloat16)


def sample_rows(sines, depth_first, depth_count, depth_total):
    number = sines.shape[0]
    depth_place = (depth_first + jnp.arange(depth_count, dtype=jnp.int32)).astype(jnp.float32)
    tilt_factor = (2.0 * depth_place - (depth_total - 1)) / (depth_total - 1)
    offset_rows = 0.5 + (HALO - 1) * sines[:, None] * tilt_factor[None, :]
    floor_part = jnp.floor(offset_rows)
    fraction = offset_rows - floor_part
    row_index = (
        HALO
        + floor_part.astype(jnp.int32)[:, :, None]
        + 2 * jnp.arange(YB_DEV, dtype=jnp.int32)[None, None, :]
    )
    row_index = row_index.reshape(number, depth_count * YB_DEV)
    fraction = jnp.broadcast_to(fraction[:, :, None], (number, depth_count, YB_DEV)).reshape(
        number, depth_count * YB_DEV
    )
    return (row_index, fraction)


def column_weights(cosines, block_index):
    block_width = min(128, NX)
    band_width = NU // NX * block_width
    x_place = (block_index * block_width + jnp.arange(block_width, dtype=jnp.int32)).astype(
        jnp.float32
    )
    column = (NU - 1) / 2.0 + NU / NX * cosines[:, None] * (x_place[None, :] - (NX - 1) / 2.0)
    first_column = jnp.minimum(column[:, 0], column[:, -1])
    band_start = jnp.clip(jnp.floor(first_column), 0, NU - band_width).astype(jnp.int32)
    columns = (band_start[:, None] + jnp.arange(band_width, dtype=jnp.int32)[None, :]).astype(
        jnp.float32
    )
    weights = jnp.maximum(0.0, 1.0 - jnp.abs(columns[:, :, None] - column[:, None, :]))
    return (band_start, weights.astype(jnp.bfloat16))


def slice_band(extended_rows, band_start):
    return lax.dynamic_slice_in_dim(extended_rows, band_start, NU // NX * min(128, NX), 1)


def take_rows(column_band, row_index):
    return jnp.take(column_band, row_index, axis=0)


def backproject(extended, cosines, sines, depth_first, depth_count, depth_total):
    row_index, fraction = sample_rows(sines, depth_first, depth_count, depth_total)
    block_width = min(128, NX)
    results = []
    for block_index in range(NX // block_width):
        band_start, weights = column_weights(cosines, block_index)
        column_band = jax.vmap(slice_band)(extended, band_start)
        low_rows = jax.vmap(take_rows)(column_band, row_index).astype(jnp.float32)
        high_rows = jax.vmap(take_rows)(column_band, row_index + 1).astype(jnp.float32)
        blended = (
            (1.0 - fraction)[:, :, None] * low_rows + fraction[:, :, None] * high_rows
        ).astype(jnp.bfloat16)
        results.append(
            jnp.einsum("pmu,pux->mx", blended, weights, preferred_element_type=jnp.float32)
        )
    return jnp.concatenate(results, axis=1)


def folded_square(indices, number):
    frequency = ((indices + number // 2) % number - number // 2).astype(jnp.float32) / number
    return frequency * frequency


def annulus_gain(radius_square):
    lower_part = (radius_square / (lower_edge * lower_edge)) ** 8
    upper_part = (radius_square / (upper_edge * upper_edge)) ** 8
    return lower_part / (1.0 + lower_part) / (1.0 + upper_part)


def wave_tables(number):
    indices = jnp.arange(number, dtype=jnp.int32)
    phase_step = indices[:, None] * indices[None, :] % number
    phase = 2.0 * math.pi * phase_step.astype(jnp.float32) / number
    return jnp.stack([jnp.cos(phase), jnp.sin(phase)])


def on_device(projections, angle_index, row_ranges):
    depth_count = lax.axis_size("depth")
    band_count = lax.axis_size("yband")
    depth_total = ZS_DEV * depth_count
    line_total = YB_DEV * band_count
    scale = math.pi / (NP_DEV * depth_count)
    extent = RB_DEV + 2 * HALO
    angles = 2.0 * math.pi * angle_index.astype(jnp.float32) / NANG
    cosines = jnp.cos(angles)
    sines = jnp.sin(angles)
    filtered = jnp.dot(
        projections.reshape(-1, NU), ramp_table(), preferred_element_type=jnp.float32
    )
    filtered = filtered.astype(jnp.bfloat16).reshape(NP_DEV, RB_DEV, NU)
    extended = padded(filtered, (("yband", 1),), HALO)
    band_index = lax.axis_index("yband")
    detector_row = band_index * RB_DEV - HALO + jnp.arange(extent, dtype=jnp.int32)
    accepted = (detector_row >= row_ranges[0, 0]) & (detector_row < row_ranges[0, 1])
    extended = extended * accepted.astype(jnp.bfloat16)[None, :, None]
    depth_index = lax.axis_index("depth")
    initial = jnp.zeros((ZS_DEV * YB_DEV, NX), jnp.float32)
    running = initial
    shards = lax.all_gather(extended, "depth", axis=0, tiled=True)
    for group_index in range(shards.shape[0] // NP_DEV):
        first_row = group_index * NP_DEV
        cos_part = lax.dynamic_slice_in_dim(cosines, first_row, NP_DEV)
        sin_part = lax.dynamic_slice_in_dim(sines, first_row, NP_DEV)
        portion = (
            backproject(
                shards[first_row : first_row + NP_DEV],
                cos_part,
                sin_part,
                depth_index * ZS_DEV,
                ZS_DEV,
                depth_total,
            )
            * scale
        )
        running = running + lax.optimization_barrier(portion.astype(jnp.bfloat16)).astype(
            jnp.float32
        )
    volume = running
    volume = volume.reshape(ZS_DEV, YB_DEV, NX)
    columns = lax.all_to_all(
        volume.astype(jnp.bfloat16), "yband", split_axis=0, concat_axis=1, tiled=True
    ).astype(volume.dtype)
    slices = columns.shape[0]
    column_tables = wave_tables(NX)
    row_tables = wave_tables(line_total)
    depth_tables = wave_tables(depth_total)
    along_columns = jnp.einsum("akx,zyx->azyk", column_tables, columns, precision=highest)
    moving = jnp.einsum("bjy,azyk->abzjk", row_tables, along_columns, precision=highest)
    moving = moving.reshape(4, slices, line_total, NX)
    row_share = line_total // (depth_count * band_count)
    gathered = lax.all_to_all(
        moving.astype(jnp.bfloat16), ("depth", "yband"), split_axis=2, concat_axis=1, tiled=True
    ).astype(moving.dtype)
    spectra = gathered.reshape(2, 2, depth_total, row_share, NX)
    along_depth = jnp.einsum("ciz,abzrk->cabirk", depth_tables, spectra, precision=highest)
    flat_index = depth_index * band_count + band_index
    row_frequency = flat_index * row_share + jnp.arange(row_share, dtype=jnp.int32)
    depth_sq = folded_square(jnp.arange(depth_total, dtype=jnp.int32), depth_total)
    row_sq = folded_square(row_frequency, line_total)
    column_sq = folded_square(jnp.arange(NX, dtype=jnp.int32), NX)
    radius_square = depth_sq[:, None, None] + row_sq[None, :, None] + column_sq[None, None, :]
    band_gain = annulus_gain(radius_square) / float(depth_total * line_total * NX)
    weighted = along_depth * band_gain[None, None, None, :, :, :]
    back_depth = jnp.einsum("ciz,cabirk->abzrk", depth_tables, weighted, precision=highest)
    back_cross = jnp.einsum("akx,abzrk->bzrx", column_tables, back_depth, precision=highest)
    returned = lax.all_to_all(
        back_cross.astype(jnp.bfloat16), ("depth", "yband"), split_axis=1, concat_axis=2, tiled=True
    ).astype(back_cross.dtype)
    return jnp.einsum("bjy,bzjx->zyx", row_tables, returned, precision=highest)


def solution(mesh):
    placed = (P("depth", "yband", None), P(), P("yband", None))
    return jax.shard_map(
        on_device,
        mesh=mesh,
        in_specs=placed,
        out_specs=P(("depth", "yband"), None, None),
        check_vma=False,
    )
```

profile of v0, /device:TPU:1, one launch (start us, length us, event | category | flops | bytes accessed | tf_op | source)
XLA Modules:
  0.0 748.5 jit_solution(16616373222521614191)
XLA Ops:
  7.4 14.0 %fusion.25 = bf16[2048,32]{0,1:T(8,128)(2,1)S(1)} fusion(bf16[32,2048]{1,0:T(8,128)(2,1)S(1)} %bitcast.803), kind=kOutput, calls=%fused_computation.225 | convolution fusion | flops 364969984 | bytes 262144 | tf_op jit(solution)/shard_map/dot_general | solution.py:142
  21.6 3.3 collective-permute-start.1
  25.1 3.5 collective-permute-start
  142.6 48.2 %all-gather.2.cloned.1.call-done = bf16[16,40,2048]{2,1,0:T(8,128)(2,1)} async-done(((bf16[2,40,2048]{2,1,0:T(8,128)(2,1)}), bf16[16,40,2048]{2,1,0:T(8,128)(2,1)}) %all-gather.2.cloned.1.call-update) | async-done | bytes 2621456 | tf_op jit(solution)/shard_map/all_gather | solution.py:154
  190.8 2.6 fusion.1343
  193.4 2.5 copy.922
  219.9 2.3 gather_fusion.71
  227.1 2.7 gather_fusion.73
  234.6 2.3 gather_fusion.75
  241.8 2.3 gather_fusion.77
  248.9 2.3 gather_fusion.78
  277.9 2.5 gather_fusion.169
  283.7 2.3 gather_fusion.171
  313.4 2.3 gather_fusion.148
  322.3 2.5 gather_fusion.153
  328.0 2.3 gather_fusion.155
  333.6 2.3 gather_fusion.157
  336.0 2.3 gather_fusion.156
  339.3 2.3 gather_fusion.158
  357.1 2.3 gather_fusion.133
  368.3 2.7 gather_fusion.137
  374.3 2.3 gather_fusion.139
  379.9 2.3 gather_fusion.141
  385.5 2.3 gather_fusion.142
  403.2 2.3 gather_fusion.117
  414.5 2.5 gather_fusion.121
  420.3 2.3 gather_fusion.123
  425.9 2.3 gather_fusion.125
  431.5 2.3 gather_fusion.126
  460.7 2.5 gather_fusion.105
  463.2 2.3 gather_fusion.104
  466.5 2.3 gather_fusion.107
  472.1 2.3 gather_fusion.109
  477.7 2.3 gather_fusion.110
  495.5 2.3 gather_fusion.85
  506.7 2.7 gather_fusion.89
  512.7 2.3 gather_fusion.91
  518.3 2.3 gather_fusion.93
  552.9 2.5 gather_fusion.185
  561.1 2.3 gather_fusion.186
  645.4 5.5 all-to-all-start
  650.9 17.5 %fusion.30 = (f32[1,1024,1024]{2,1,0:T(8,128)}, f32[1,1024,1024]{2,1,0:T(8,128)}) fusion(), kind=kLoop, calls=%fused_computation.228 | loop fusion | flops 14680064 | bytes 8388608 | tf_op jit(solution)/shard_map/sin | solution.py:129
  668.7 8.1 %fusion.32 = f32[2,128,1024,1]{2,1,3,0:T(8,128)S(1)} fusion(f32[1,1024,1024]{2,1,0:T(8,128)} %get-tuple-element.320, f32[1,1024,1024]{2,1,0:T(8,128)} %get-tuple-element.321, bf16[16,8,1024]{2,1,0:T(8,128)(2,1)S(1)} %all-to-all-done), kind=kOutput, calls=%fused_computation.231 | convolution fusion | flops 3223322624 | bytes 9699328 | tf_op jit(solution)/shard_map/akx,zyx->azyk/dot_general | solution.py:182
  680.4 6.8 all-to-all-start.1
  687.6 19.1 %all-to-all-done.1 = bf16[4,1,128,1024]{3,0,1,2:T(4,128)(2,1)S(1)} async-done(((bf16[4,1,128,1024]{3,0,1,2:T(4,128)(2,1)}), bf16[4,1,128,1024]{3,0,1,2:T(4,128)(2,1)S(1)}, u32[]{:S(2)}, u32[]{:S(2)}) %all-to-all-start.1) | async-done | bytes 1048608 | tf_op jit(solution)/shard_map/all_to_all | solution.py:186
  709.8 3.4 fusion.20
  713.2 7.5 %fusion.43 = bf16[2,128,1,1024]{3,1,0,2:T(8,128)(2,1)S(1)} fusion(f32[1,1024,1024]{2,1,0:T(8,128)S(1)} %copy-done.2, f32[1,1024,1024]{2,1,0:T(8,128)S(1)} %copy-done.3, f32[2,2,1024,128,1]{3,2,4,1,0:T(8,128)S(1)} %fusion.20), kind=kOutput, calls=%fused_computation.234 | convolution fusion | flops 6444810240 | bytes 11010048 | tf_op jit(solution)/shard_map/akx,abzrk->bzrx/dot_general | solution.py:200
  721.3 17.7 %all_to_all.12 = bf16[2,128,1,1024]{3,0,2,1:T(2,128)(2,1)S(1)} all-to-all(bf16[2,128,1,1024]{3,0,2,1:T(2,128)(2,1)S(1)} %copy.909), channel_id=1, replica_groups=mesh['depth'=8,'yband'=16] {'depth','yband'}, dimensions={1} | all-to-all | bytes 1048576 | tf_op jit(solution)/shard_map/all_to_all | solution.py:201
  (1163 shorter events, 487.7 us)
Async XLA Ops:
  6.5 184.3 %all-gather.2.cloned.1.call-start = ((), (), s32[]{:S(2)}) async-start(), calls=%async_computation.3 | async-start | bytes 2949120 | tf_op jit(solution)/shard_map/all_gather | solution.py:154
  7.4 21.3 %copy-start.325 = (s32[16]{0:T(128)S(1)}, s32[16]{0:T(128)}, u32[]{:S(2)}) copy-start(s32[16]{0:T(128)} %param.6) | copy-start | bytes 196
  7.4 21.6 %copy-start.312 = (s32[1,2]{1,0:T(1,128)S(1)}, s32[1,2]{1,0:T(1,128)}, u32[]{:S(2)}) copy-start(s32[1,2]{1,0:T(1,128)} %param.7) | copy-start | bytes 28
  21.6 106.6 %collective-permute-start.1 = (bf16[2,12,2048]{2,0,1:T(2,128)(2,1)S(1)}, bf16[2,12,2048]{2,0,1:T(2,128)(2,1)S(1)}, u32[]{:S(2)}, u32[]{:S(2)}) collective-permute-start(bf16[2,12,2048]{2,0,1:T(2,128)(2,1)S(1)} %copy.921), channel_id=1, source_target_pairs={{1,0},{2,1},{3,2},{4,3},{5,4},{6,5},{7,6},{8,7},{9,8},{10,9},{11,1... | collective-permute-start | bytes 294920 | tf_op jit(solution)/shard_map/ppermute | solution.py:33
  25.1 103.2 %collective-permute-start = (bf16[2,12,2048]{2,0,1:T(2,128)(2,1)S(1)}, bf16[2,12,2048]{2,0,1:T(2,128)(2,1)S(1)}, u32[]{:S(2)}, u32[]{:S(2)}) collective-permute-start(bf16[2,12,2048]{2,0,1:T(2,128)(2,1)S(1)} %copy.920), channel_id=1, source_target_pairs={{0,1},{1,2},{2,3},{3,4},{4,5},{5,6},{6,7},{7,8},{8,9},{9,10},{10,1... | collective-permute-start | bytes 294920 | tf_op jit(solution)/shard_map/ppermute | solution.py:31
  38.1 89.9 %copy-start.129 = (f32[2,128]{1,0:T(2,128)}, f32[2,128]{1,0:T(2,128)S(1)}, u32[]{:S(2)}) copy-start(f32[2,128]{1,0:T(2,128)S(1)} %get-tuple-element.234) | copy-start | bytes 3076
  38.1 89.9 %copy-start.131 = (f32[2,128]{1,0:T(2,128)}, f32[2,128]{1,0:T(2,128)S(1)}, u32[]{:S(2)}) copy-start(f32[2,128]{1,0:T(2,128)S(1)} %get-tuple-element.236) | copy-start | bytes 3076
  38.1 89.9 %copy-start.133 = (f32[2,128]{1,0:T(2,128)}, f32[2,128]{1,0:T(2,128)S(1)}, u32[]{:S(2)}) copy-start(f32[2,128]{1,0:T(2,128)S(1)} %get-tuple-element.238) | copy-start | bytes 3076
  38.1 89.9 %copy-start.135 = (f32[2,128]{1,0:T(2,128)}, f32[2,128]{1,0:T(2,128)S(1)}, u32[]{:S(2)}) copy-start(f32[2,128]{1,0:T(2,128)S(1)} %get-tuple-element.232) | copy-start | bytes 3076
  38.1 89.9 %copy-start.137 = (f32[2,128]{1,0:T(2,128)}, f32[2,128]{1,0:T(2,128)S(1)}, u32[]{:S(2)}) copy-start(f32[2,128]{1,0:T(2,128)S(1)} %get-tuple-element.179) | copy-start | bytes 3076
  38.1 89.9 %copy-start.139 = (f32[2,128]{1,0:T(2,128)}, f32[2,128]{1,0:T(2,128)S(1)}, u32[]{:S(2)}) copy-start(f32[2,128]{1,0:T(2,128)S(1)} %get-tuple-element.180) | copy-start | bytes 3076
  38.2 89.9 %copy-start.141 = (f32[2,128]{1,0:T(2,128)}, f32[2,128]{1,0:T(2,128)S(1)}, u32[]{:S(2)}) copy-start(f32[2,128]{1,0:T(2,128)S(1)} %get-tuple-element.194) | copy-start | bytes 3076
  38.2 89.9 %copy-start.143 = (f32[2,128]{1,0:T(2,128)}, f32[2,128]{1,0:T(2,128)S(1)}, u32[]{:S(2)}) copy-start(f32[2,128]{1,0:T(2,128)S(1)} %get-tuple-element.216) | copy-start | bytes 3076
  38.2 89.9 %copy-start.145 = (f32[2,128]{1,0:T(2,128)}, f32[2,128]{1,0:T(2,128)S(1)}, u32[]{:S(2)}) copy-start(f32[2,128]{1,0:T(2,128)S(1)} %get-tuple-element.204) | copy-start | bytes 3076
  38.2 89.9 %copy-start.147 = (f32[2,128]{1,0:T(2,128)}, f32[2,128]{1,0:T(2,128)S(1)}, u32[]{:S(2)}) copy-start(f32[2,128]{1,0:T(2,128)S(1)} %get-tuple-element.186) | copy-start | bytes 3076
  38.2 89.9 %copy-start.149 = (f32[2,128]{1,0:T(2,128)}, f32[2,128]{1,0:T(2,128)S(1)}, u32[]{:S(2)}) copy-start(f32[2,128]{1,0:T(2,128)S(1)} %get-tuple-element.178) | copy-start | bytes 3076
  38.2 89.9 %copy-start.151 = (f32[2,128]{1,0:T(2,128)}, f32[2,128]{1,0:T(2,128)S(1)}, u32[]{:S(2)}) copy-start(f32[2,128]{1,0:T(2,128)S(1)} %get-tuple-element.230) | copy-start | bytes 3076
  38.2 89.9 %copy-start.153 = (f32[2,128]{1,0:T(2,128)}, f32[2,128]{1,0:T(2,128)S(1)}, u32[]{:S(2)}) copy-start(f32[2,128]{1,0:T(2,128)S(1)} %get-tuple-element.184) | copy-start | bytes 3076
  38.2 89.9 %copy-start.155 = (f32[2,128]{1,0:T(2,128)}, f32[2,128]{1,0:T(2,128)S(1)}, u32[]{:S(2)}) copy-start(f32[2,128]{1,0:T(2,128)S(1)} %get-tuple-element.182) | copy-start | bytes 3076
  38.2 89.9 %copy-start.159 = (f32[2,128]{1,0:T(2,128)}, f32[2,128]{1,0:T(2,128)S(1)}, u32[]{:S(2)}) copy-start(f32[2,128]{1,0:T(2,128)S(1)} %get-tuple-element.215) | copy-start | bytes 3076
  38.2 89.9 %copy-start.161 = (f32[2,128]{1,0:T(2,128)}, f32[2,128]{1,0:T(2,128)S(1)}, u32[]{:S(2)}) copy-start(f32[2,128]{1,0:T(2,128)S(1)} %get-tuple-element.203) | copy-start | bytes 3076
  38.3 89.9 %copy-start.163 = (f32[2,128]{1,0:T(2,128)}, f32[2,128]{1,0:T(2,128)S(1)}, u32[]{:S(2)}) copy-start(f32[2,128]{1,0:T(2,128)S(1)} %get-tuple-element.185) | copy-start | bytes 3076
  38.3 89.9 %copy-start.165 = (f32[2,128]{1,0:T(2,128)}, f32[2,128]{1,0:T(2,128)S(1)}, u32[]{:S(2)}) copy-start(f32[2,128]{1,0:T(2,128)S(1)} %get-tuple-element.183) | copy-start | bytes 3076
  38.3 89.9 %copy-start.167 = (f32[2,128]{1,0:T(2,128)}, f32[2,128]{1,0:T(2,128)S(1)}, u32[]{:S(2)}) copy-start(f32[2,128]{1,0:T(2,128)S(1)} %get-tuple-element.229) | copy-start | bytes 3076
  38.3 89.9 %copy-start.169 = (f32[2,128]{1,0:T(2,128)}, f32[2,128]{1,0:T(2,128)S(1)}, u32[]{:S(2)}) copy-start(f32[2,128]{1,0:T(2,128)S(1)} %get-tuple-element.191) | copy-start | bytes 3076
  38.3 89.9 %copy-start.171 = (f32[2,128]{1,0:T(2,128)}, f32[2,128]{1,0:T(2,128)S(1)}, u32[]{:S(2)}) copy-start(f32[2,128]{1,0:T(2,128)S(1)} %get-tuple-element.189) | copy-start | bytes 3076
  38.3 89.9 %copy-start.173 = (f32[2,128]{1,0:T(2,128)}, f32[2,128]{1,0:T(2,128)S(1)}, u32[]{:S(2)}) copy-start(f32[2,128]{1,0:T(2,128)S(1)} %get-tuple-element.192) | copy-start | bytes 3076
  38.3 89.9 %copy-start.175 = (f32[2,128]{1,0:T(2,128)}, f32[2,128]{1,0:T(2,128)S(1)}, u32[]{:S(2)}) copy-start(f32[2,128]{1,0:T(2,128)S(1)} %get-tuple-element.214) | copy-start | bytes 3076
  38.3 89.9 %copy-start.177 = (f32[2,128]{1,0:T(2,128)}, f32[2,128]{1,0:T(2,128)S(1)}, u32[]{:S(2)}) copy-start(f32[2,128]{1,0:T(2,128)S(1)} %get-tuple-element.202) | copy-start | bytes 3076
  38.3 89.9 %copy-start.179 = (f32[2,128]{1,0:T(2,128)}, f32[2,128]{1,0:T(2,128)S(1)}, u32[]{:S(2)}) copy-start(f32[2,128]{1,0:T(2,128)S(1)} %get-tuple-element.188) | copy-start | bytes 3076
  38.3 89.9 %copy-start.181 = (f32[2,128]{1,0:T(2,128)}, f32[2,128]{1,0:T(2,128)S(1)}, u32[]{:S(2)}) copy-start(f32[2,128]{1,0:T(2,128)S(1)} %get-tuple-element.190) | copy-start | bytes 3076
  38.4 89.9 %copy-start.183 = (f32[2,128]{1,0:T(2,128)}, f32[2,128]{1,0:T(2,128)S(1)}, u32[]{:S(2)}) copy-start(f32[2,128]{1,0:T(2,128)S(1)} %get-tuple-element.228) | copy-start | bytes 3076
  38.4 89.9 %copy-start.185 = (f32[2,128]{1,0:T(2,128)}, f32[2,128]{1,0:T(2,128)S(1)}, u32[]{:S(2)}) copy-start(f32[2,128]{1,0:T(2,128)S(1)} %get-tuple-element.200) | copy-start | bytes 3076
  38.4 89.9 %copy-start.187 = (f32[2,128]{1,0:T(2,128)}, f32[2,128]{1,0:T(2,128)S(1)}, u32[]{:S(2)}) copy-start(f32[2,128]{1,0:T(2,128)S(1)} %get-tuple-element.198) | copy-start | bytes 3076
  38.4 89.9 %copy-start.189 = (f32[2,128]{1,0:T(2,128)}, f32[2,128]{1,0:T(2,128)S(1)}, u32[]{:S(2)}) copy-start(f32[2,128]{1,0:T(2,128)S(1)} %get-tuple-element.196) | copy-start | bytes 3076
  38.4 89.9 %copy-start.191 = (f32[2,128]{1,0:T(2,128)}, f32[2,128]{1,0:T(2,128)S(1)}, u32[]{:S(2)}) copy-start(f32[2,128]{1,0:T(2,128)S(1)} %get-tuple-element.213) | copy-start | bytes 3076
  38.4 89.9 %copy-start.193 = (f32[2,128]{1,0:T(2,128)}, f32[2,128]{1,0:T(2,128)S(1)}, u32[]{:S(2)}) copy-start(f32[2,128]{1,0:T(2,128)S(1)} %get-tuple-element.201) | copy-start | bytes 3076
  38.4 104.1 %copy-start.157 = (f32[2,128]{1,0:T(2,128)}, f32[2,128]{1,0:T(2,128)S(1)}, u32[]{:S(2)}) copy-start(f32[2,128]{1,0:T(2,128)S(1)} %get-tuple-element.193) | copy-start | bytes 3076
  38.4 104.1 %copy-start.195 = (f32[2,128]{1,0:T(2,128)}, f32[2,128]{1,0:T(2,128)S(1)}, u32[]{:S(2)}) copy-start(f32[2,128]{1,0:T(2,128)S(1)} %get-tuple-element.197) | copy-start | bytes 3076
  38.4 104.1 %copy-start.197 = (f32[2,128]{1,0:T(2,128)}, f32[2,128]{1,0:T(2,128)S(1)}, u32[]{:S(2)}) copy-start(f32[2,128]{1,0:T(2,128)S(1)} %get-tuple-element.199) | copy-start | bytes 3076
  38.4 104.1 %copy-start.199 = (f32[2,128]{1,0:T(2,128)}, f32[2,128]{1,0:T(2,128)S(1)}, u32[]{:S(2)}) copy-start(f32[2,128]{1,0:T(2,128)S(1)} %get-tuple-element.227) | copy-start | bytes 3076
  38.5 104.1 %copy-start.201 = (f32[2,128]{1,0:T(2,128)}, f32[2,128]{1,0:T(2,128)S(1)}, u32[]{:S(2)}) copy-start(f32[2,128]{1,0:T(2,128)S(1)} %get-tuple-element.211) | copy-start | bytes 3076
  38.5 104.1 %copy-start.203 = (f32[2,128]{1,0:T(2,128)}, f32[2,128]{1,0:T(2,128)S(1)}, u32[]{:S(2)}) copy-start(f32[2,128]{1,0:T(2,128)S(1)} %get-tuple-element.209) | copy-start | bytes 3076
  38.5 104.1 %copy-start.205 = (f32[2,128]{1,0:T(2,128)}, f32[2,128]{1,0:T(2,128)S(1)}, u32[]{:S(2)}) copy-start(f32[2,128]{1,0:T(2,128)S(1)} %get-tuple-element.207) | copy-start | bytes 3076
  205.6 18.9 %copy-start.262 = (s32[2]{0:T(128)S(1)}, s32[2]{0:T(128)}, u32[]{:S(2)}) copy-start(s32[2]{0:T(128)} %get-tuple-element.13) | copy-start | bytes 28
  645.4 23.3 %all-to-all-start = ((bf16[16,8,1024]{2,1,0:T(8,128)(2,1)}), bf16[16,8,1024]{2,1,0:T(8,128)(2,1)S(1)}, u32[]{:S(2)}, u32[]{:S(2)}) async-start(bf16[16,8,1024]{2,1,0:T(8,128)(2,1)} %bitcast.454), calls=%async_computation | async-start | bytes 524288 | tf_op jit(solution)/shard_map/all_to_all | solution.py:175
  680.4 26.3 %all-to-all-start.1 = ((bf16[4,1,128,1024]{3,0,1,2:T(4,128)(2,1)}), bf16[4,1,128,1024]{3,0,1,2:T(4,128)(2,1)S(1)}, u32[]{:S(2)}, u32[]{:S(2)}) async-start(bf16[4,1,128,1024]{3,0,1,2:T(4,128)(2,1)} %copy.906), calls=%async_computation.1 | async-start | bytes 2097152 | tf_op jit(solution)/shard_map/all_to_all | solution.py:186
  713.2 28.0 %copy-start.1 = (bf16[2,16,2048]{2,1,0:T(8,128)(2,1)S(1)}, bf16[2,16,2048]{2,1,0:T(8,128)(2,1)}, u32[]{:S(2)}) copy-start(bf16[2,16,2048]{2,1,0:T(8,128)(2,1)} %param.5) | copy-start | bytes 393220
  (283 other events, 2817.0 us)
Sparse Core Ops, SparseCore 0:
  129.4 61.4 all-gather.1
where the time goes:
time: 757 us; the launch traced here: 748 us
  local copies, waits for them, and re-layouts  394 us (52%)
  other arithmetic  128 us (17%)
  matrix products  102 us (13%)
  waiting for transfers between devices  67.4 us (9%)
  between operations  19.8 us (3%)
  starting transfers between devices  19.2 us (3%)
  blocking collectives  17.7 us (2%)
    gather x128, local copies, waits for them, and re-layouts, take_rows(): return jnp.take(column_band, row_index, axis=0)  295 us
    gather x128, local copies, waits for them, and re-layouts, slice_band(): lax.dynamic_slice_in_dim(extended_rows, band_start, NU // NX * min(128, N...  74.9 us
    dot_general x64, matrix products, backproject(): jnp.einsum('pmu,pux->mx', blended, weights, preferred_element_type=jnp.fl...  64.6 us
    convert_element_type x64, other arithmetic, column_weights(): jnp.clip(jnp.floor(first_column), 0, NU - band_width).astype(jnp.int32)  59.1 us
    all_gather x1, waiting for transfers between devices, on_device(): shards = lax.all_gather(extended, 'depth', axis=0, tiled=True)  48.2 us
    convert_element_type x64, other arithmetic, column_weights(): (band_start[:, None] + jnp.arange(band_width, dtype=jnp.int32)[None, :])....  41.6 us
    all_to_all x1, waiting for transfers between devices, on_device(): lax.all_to_all(moving.astype(jnp.bfloat16), ('depth', 'yband'), split_axi...  19.1 us
    sin x2, other arithmetic, wave_tables(): return jnp.stack([jnp.cos(phase), jnp.sin(phase)])  17.8 us
  transfers between devices with their start and end apart: 5, of which 2 were waited for; matrix products, arithmetic and copies ran while one was open for 17% of the time, Pallas kernels for 0%

commit v1 on v0

v1 whole, which is shorter than its diff:
```python
import math

import jax
import jax.numpy as jnp
import numpy as np
from jax import lax
from jax.experimental import pallas as pl
from jax.experimental.pallas import tpu as pltpu
from jax.sharding import PartitionSpec as P

NX, NU, NANG, NY, NZ = 1024, 2048, 1440, 128, 128
NP_DEV, YB, RB, HALO, BANDS, NPROJ = 2, 8, 16, 12, 16, 16
N = 128
KX = NX // N
MESH = pl.DeviceIdType.MESH
highest = lax.Precision.HIGHEST
lower_edge, upper_edge = 0.04, 0.35


def real_basis(n):
    t = np.arange(n)
    rows = np.arange(n)
    k = np.where(rows <= n // 2, rows, rows - n // 2)
    ph = 2.0 * np.pi * ((k[:, None] * t[None, :]) % n) / n
    q = np.where((rows <= n // 2)[:, None], np.cos(ph), np.sin(ph))
    norm = np.where((rows == 0) | (rows == n // 2), 1.0 / n, 2.0 / n)
    return q * np.sqrt(norm)[:, None], k


def ramp_values():
    n = np.arange(-(NU - 1), NU)
    odd = n % 2 != 0
    d = np.where(odd, n, 1).astype(np.float32)
    v = np.where(n == 0, np.float32(0.25), np.where(odd, np.float32(-1.0) / (np.float32(math.pi * math.pi) * d * d), np.float32(0)))
    return (v / np.float32(NX / NU)).astype(jnp.bfloat16)


def exchange(x, cid, name):
    def kernel(x_ref, o_ref, ss, rs):
        me = lax.axis_index("depth") * BANDS + lax.axis_index("yband")

        def place(o):
            t = (me + o) & (N - 1)
            return t, (t >> 4, t & 15)

        bar = pltpu.get_barrier_semaphore()

        def greet(o, c):
            pl.semaphore_signal(bar, inc=1, device_id=place(o)[1], device_id_type=MESH)
            return c

        lax.fori_loop(1, N, greet, 0)
        pl.semaphore_wait(bar, N - 1)

        def send(o, c):
            t, dev = place(o)
            pltpu.make_async_remote_copy(x_ref.at[t], o_ref.at[me], ss, rs, device_id=dev, device_id_type=MESH).start()
            return c

        lax.fori_loop(1, N, send, 0)
        o_ref[me] = x_ref[me]
        pltpu.make_async_copy(x_ref.at[pl.ds(0, N - 1)], x_ref.at[pl.ds(0, N - 1)], ss).wait()
        pltpu.make_async_copy(o_ref.at[pl.ds(0, N - 1)], o_ref.at[pl.ds(0, N - 1)], rs).wait()

    return pl.pallas_call(
        kernel,
        name=name,
        out_shape=jax.ShapeDtypeStruct(x.shape, x.dtype),
        in_specs=[pl.BlockSpec(memory_space=pltpu.VMEM)],
        out_specs=pl.BlockSpec(memory_space=pltpu.VMEM),
        scratch_shapes=[pltpu.SemaphoreType.DMA, pltpu.SemaphoreType.DMA],
        compiler_params=pltpu.CompilerParams(collective_id=cid, has_side_effects=True, vmem_limit_bytes=16 * 2**20),
    )(x)


def on_device(projections, angle_index, row_ranges):
    d = lax.axis_index("depth")
    b = lax.axis_index("yband")
    me = d * BANDS + b
    theta = 2.0 * math.pi * angle_index.astype(jnp.float32) / NANG
    cosines, sines = jnp.cos(theta), jnp.sin(theta)
    qx, kx = real_basis(NX)
    qy, ky = real_basis(NY)
    qz, kz = real_basis(NZ)
    v = ramp_values()
    idx = np.arange(NU)[:, None] - np.arange(NU)[None, :] + NU - 1
    ramp = jnp.asarray(v[idx])
    filtered = jnp.dot(projections.reshape(-1, NU), ramp, preferred_element_type=jnp.float32)
    filtered = filtered.astype(jnp.bfloat16).reshape(NP_DEV, RB, NU)
    cos_own = lax.dynamic_slice_in_dim(cosines, d * NP_DEV, NP_DEV)
    x = jnp.arange(NX, dtype=jnp.float32)
    column = (NU - 1) / 2.0 + NU / NX * cos_own[:, None] * (x[None, :] - (NX - 1) / 2.0)
    u = jnp.arange(NU, dtype=jnp.float32)
    w = jnp.maximum(0.0, 1.0 - jnp.abs(u[None, :, None] - column[:, None, :])).astype(jnp.bfloat16)
    g = jnp.einsum("pgu,pux->pgx", filtered, w, preferred_element_type=jnp.float32).reshape(32, NX)
    perm = (np.arange(N)[None, :] * KX + np.arange(KX)[:, None]).reshape(-1)
    qxf = jnp.asarray(qx.T[:, perm].astype(np.float32))
    ghat = jnp.dot(g, qxf, precision=highest)
    s = ghat.reshape(32, KX, N).transpose(2, 1, 0).reshape(N, 256)
    lane = jnp.arange(128)
    lim = jnp.where(lane < 64, row_ranges[0, 0], row_ranges[0, 1])
    lim = jnp.where(lane % 16 == b, lim, 0).astype(jnp.float32)
    s = jnp.concatenate([s, jnp.broadcast_to(lim[None], (N, 128))], axis=1)
    r = exchange(s.reshape(N, 1, 384), 1, "spectra").reshape(N, 384)
    lims = r[:16, 256:].sum(0)
    lo = jnp.tile(lims[:16], KX)
    hi = jnp.tile(lims[64:80], KX)
    dd = r[:, :256].reshape(8, BANDS, KX, 32).transpose(0, 3, 2, 1).reshape(256, 128)
    grow = jnp.tile(jnp.arange(16), 16)
    blocks = []
    for sh in (-1, 0, 1):
        row = (16 * (jnp.tile(jnp.arange(16), KX)[None, :] + sh) + grow[:, None]).astype(jnp.float32)
        ok = (row >= lo) & (row < hi) & (row >= 0) & (row < 256)
        blocks.append(jnp.where(ok, jnp.roll(dd, -sh, axis=1), 0.0))
    dext = jnp.concatenate(blocks, axis=0).astype(jnp.bfloat16)
    sin_l = jnp.tile(jnp.repeat(sines, 16), 3)
    c_l = (16 * (jnp.arange(768) // 256) - 16 + jnp.arange(768) % 16).astype(jnp.float32)
    tilt = (2.0 * jnp.arange(NZ, dtype=jnp.float32) - (NZ - 1)) / (NZ - 1)
    e = c_l[None] - (0.5 + (HALO - 1) * sin_l[None] * tilt[:, None])
    parts = []
    for yy in range(YB):
        rm = jnp.maximum(0.0, 1.0 - jnp.abs(e - 2.0 * yy)).astype(jnp.bfloat16)
        parts.append(jnp.dot(rm, dext, preferred_element_type=jnp.float32))
    vol = jnp.concatenate(parts, axis=1)
    bt = np.zeros((YB, KX, BANDS, KX, NY))
    for kk in range(KX):
        bt[:, kk, :, kk, :] = qy.reshape(NY, BANDS, YB).transpose(2, 1, 0)
    bt = jnp.asarray(bt.reshape(1024, 1024).astype(np.float32))
    t1 = jnp.dot(vol, bt, precision=highest)
    qzc = jnp.asarray(qz.astype(np.float32))
    t2 = jnp.dot(qzc, t1, precision=highest)
    row = me * KX + jnp.arange(KX)
    fx = (jnp.where(row <= NX // 2, row, row - NX // 2).astype(jnp.float32) / NX) ** 2
    fy = jnp.asarray(((ky / NY) ** 2).astype(np.float32))
    fz = jnp.asarray(((kz / NZ) ** 2).astype(np.float32))
    rad = fz[:, None] + (fx[:, None] + fy[None, :]).reshape(1, 1024)
    low = (rad / (lower_edge * lower_edge)) ** 8
    up = (rad / (upper_edge * upper_edge)) ** 8
    gain = low / (1.0 + low) / (1.0 + up) * (math.pi / NPROJ)
    t3 = jnp.dot(qzc.T, t2 * gain, precision=highest)
    t4 = jnp.einsum("zkj,jy->zky", t3.reshape(NZ, KX, NY), jnp.asarray(qy.astype(np.float32)), precision=highest)
    back = exchange(t4.astype(jnp.bfloat16), 2, "volume").reshape(NX, NY)
    out = lax.dot_general(back.astype(jnp.float32), jnp.asarray(qx.astype(np.float32)), (((0,), (0,)), ((), ())), precision=highest)
    return out[None]


def solution(mesh):
    return jax.shard_map(
        on_device,
        mesh=mesh,
        in_specs=(P("depth", "yband", None), P(), P("yband", None)),
        out_specs=P(("depth", "yband"), None, None),
        check_vma=False,
    )
```

time: 757 us -> 60.6 us (0.08); the launches traced: 748 us -> 60.4 us
  local copies, waits for them, and re-layouts: 394 us -> 3.91 us
  other arithmetic: 128 us -> 3.08 us
  matrix products: 102 us -> 22.9 us
  waiting for transfers between devices: 67.4 us -> 0 us
  Pallas kernels: 0 us -> 30 us
  between operations: 19.8 us -> 0.48 us
  starting transfers between devices: 19.2 us -> 0 us
  blocking collectives: 17.7 us -> 0 us
    gather x256 -> x0, local copies, waits for them, and re-layouts: 370 us -> none  [the longest x128 295 us: take_rows(): return jnp.take(column_band, row_index, axis=0)]
    convert_element_type x138 -> x2, other arithmetic: 103 us -> 1.2 us  [the longest x1 1.19 us: on_device(): lim = jnp.where(lane % 16 == b, lim, 0).astype(jnp.float32)]
    dot_general x71 -> x23, matrix products: 102 us -> 22.9 us  [the longest x1 4.93 us: on_device(): jnp.dot(projections.reshape(-1, NU), ramp, preferred_element_type=jnp.flo...]
    all_gather x1 -> x0, waiting for transfers between devices: 48.2 us -> none  [on_device(): shards = lax.all_gather(extended, 'depth', axis=0, tiled=True)]
    pallas_call x0 -> x2, Pallas kernels: none -> 30 us  [exchange(): pl.pallas_call(kernel, name=name, out_shape=jax.ShapeDtypeStruct(x.shape,...]
    all_to_all x2 -> x0, waiting for transfers between devices: 19.1 us -> none  [the longest x1 19.1 us: on_device(): lax.all_to_all(moving.astype(jnp.bfloat16), ('depth', 'yband'), split_axi...]
    sin x3 -> x0, other arithmetic: 17.8 us -> none  [the longest x2 17.8 us: wave_tables(): return jnp.stack([jnp.cos(phase), jnp.sin(phase)])]
    all_to_all x1 -> x0, blocking collectives: 17.7 us -> none  [on_device(): lax.all_to_all(back_cross.astype(jnp.bfloat16), ('depth', 'yband'), split...]
  transfers between devices with their start and end apart: 5 -> 0, of which waited for: 2 -> 0; matrix products, arithmetic and copies ran while one was open for 17% -> 0% of each run, Pallas kernels for 0% -> 0%
where the time goes in v1:
time: 60.6 us; the launch traced here: 60.4 us
  Pallas kernels  30 us (50%)
  matrix products  22.9 us (38%)
  local copies, waits for them, and re-layouts  3.91 us (6%)
  other arithmetic  3.08 us (5%)
    pallas_call x2, Pallas kernels, exchange(): pl.pallas_call(kernel, name=name, out_shape=jax.ShapeDtypeStruct(x.shape,...  30 us
    dot_general x1, matrix products, on_device(): jnp.dot(projections.reshape(-1, NU), ramp, preferred_element_type=jnp.flo...  4.93 us
    dot_general x8, matrix products, on_device(): t1 = jnp.dot(vol, bt, precision=highest)  4.64 us
    dot_general x1, matrix products, on_device(): ghat = jnp.dot(g, qxf, precision=highest)  3.92 us
    dot_general x1, matrix products, on_device(): jnp.einsum('pgu,pux->pgx', filtered, w, preferred_element_type=jnp.float32)  2.79 us
    dot_general x1, matrix products, on_device(): lax.dot_general(back.astype(jnp.float32), jnp.asarray(qx.astype(np.float3...  2.42 us
    dot_general x8, matrix products, on_device(): parts.append(jnp.dot(rm, dext, preferred_element_type=jnp.float32))  2.24 us
    slice x1, local copies, waits for them, and re-layouts, on_device(): lim = jnp.where(lane < 64, row_ranges[0, 0], row_ranges[0, 1])  1.28 us

profile of v1, /device:TPU:1, one launch (start us, length us, event | category | flops | bytes accessed | tf_op | source)
XLA Modules:
  0.0 60.4 jit_solution(1978311201000786493)
XLA Ops:
  0.0 0.9 %copy-done = bf16[2,16,2048]{2,1,0:T(8,128)(2,1)S(1)} copy-done((bf16[2,16,2048]{2,1,0:T(8,128)(2,1)S(1)}, bf16[2,16,2048]{2,1,0:T(8,128)(2,1)}, u32[]{:S(2)}) %copy-start) | copy-done | bytes 131096
  0.9 0.7 %fusion.101 = (f32[16]{0:T(128)S(1)}, f32[16]{0:T(128)S(1)}) fusion(s32[16]{0:T(128)} %param.12), kind=kLoop, calls=%fused_computation.165 | loop fusion | flops 48 | bytes 192 | tf_op jit(solution)/shard_map/cos | solution.py:81
  1.6 0.1 dynamic-slice_multiply_fusion
  1.7 1.3 %fusion.138 = (s32[1,1]{1,0:T(1,128)}, s32[1,1]{1,0:T(1,128)}) fusion(s32[1,2]{1,0:T(1,128)} %param.13), kind=kLoop, calls=%fused_computation.202 | loop fusion | bytes 16 | tf_op jit(solution)/shard_map/slice | solution.py:101
  3.0 1.2 %fusion.100 = f32[128]{0:T(128)S(1)} fusion(s32[]{:T(128)} %bitcast.8, s32[]{:T(128)} %bitcast.7, s32[]{:T(128)S(6)} %axis_index.25), kind=kLoop, calls=%fused_computation.160 | loop fusion | flops 1408 | bytes 524 | tf_op jit(solution)/shard_map/convert_element_type | solution.py:102
  4.2 0.7 %add_bitcast_fusion = f32[1024]{0:T(1024)S(1)} fusion(f32[128]{0:T(128)} %constant.148.clone, f32[8]{0:T(128)S(1)} %fusion.99), kind=kLoop, calls=%fused_computation.143 | loop fusion | flops 1024 | bytes 4640 | tf_op jit(solution)/shard_map/add | solution.py:136
  4.9 0.1 mul.187
  5.0 0.1 multiply_add_fusion
  5.1 0.1 mul.194
  5.2 0.1 mul.196
  5.3 0.1 broadcast_in_dim.20
  5.3 0.1 mul.179
  5.5 0.1 add.291
  5.5 4.9 %convolution_convert_fusion = bf16[2048,32]{0,1:T(8,128)(2,1)S(1)} fusion(bf16[32,2048]{1,0:T(8,128)(2,1)S(1)} %bitcast.61, bf16[2048,2048]{1,0:T(8,128)(2,1)} %constant.144.clone), kind=kOutput, calls=%fused_computation.2 | convolution fusion | flops 268500992 | bytes 8650752 | tf_op jit(solution)/shard_map/dot_general | solution.py:88
  10.5 2.8 %fusion = f32[2,16,1024]{2,1,0:T(8,128)S(1)} fusion(bf16[2,16,2048]{2,1,0:T(8,128)(2,1)S(1)} %bitcast.67, f32[2,1024]{1,0:T(2,128)S(1)} %multiply_add_fusion), kind=kOutput, calls=%fused_computation.1 | convolution fusion | flops 155189248 | bytes 270336 | tf_op jit(solution)/shard_map/pgu,pux->pgx/dot_general | solution.py:95
  13.3 3.9 %fusion.139 = f32[32,8,128]{2,0,1:T(8,128)S(1)} fusion(f32[32,1024,1]{1,0,2:T(8,128)S(1)} %bitcast.68, f32[8,128,1024]{2,1,0:T(8,128)S(1)} %copy-done.2), kind=kOutput, calls=%fused_computation.203 | convolution fusion | flops 402653184 | bytes 4456448 | tf_op jit(solution)/shard_map/dot_general | solution.py:98
  17.2 0.1 copy.15
  17.4 0.1 reshape.192.x_ref
  17.5 16.8 %spectra.1 = f32[128,1,384]{2,1,0:T(1,128)S(1)} custom-call(f32[128,1,384]{2,1,0:T(1,128)S(1)} %reshape.192.x_ref), custom_call_target="tpu_custom_call" | custom-call | tf_op jit(solution)/shard_map/spectra/pallas_call | solution.py:65
  34.4 0.1 fusion.137
  34.5 0.1 ge.31
  34.6 0.1 lt.61
  34.7 0.2 reshape.194
  34.8 0.2 copy.25
  35.0 0.2 reshape.195
  35.3 0.2 fusion.76
  35.5 0.3 fusion.14
  35.8 0.3 fusion.15
  36.1 0.3 fusion.16
  36.4 0.3 fusion.17
  36.7 0.3 fusion.18
  37.0 0.3 fusion.19
  37.3 0.3 fusion.20
  37.6 0.3 fusion.13
  37.9 0.6 fusion.140
  38.5 0.6 convolution_add_fusion.6
  39.1 0.6 convolution_add_fusion.5
  39.7 0.6 convolution_add_fusion.4
  40.3 0.6 convolution_add_fusion.3
  40.9 0.6 convolution_add_fusion.2
  41.5 0.6 convolution_add_fusion.1
  42.1 0.6 convolution_add_fusion
  42.7 0.8 %convolution_multiply_fusion = f32[128,1024]{1,0:T(8,128)S(1)} fusion(f32[128,128]{1,0:T(8,128)S(1)} %copy-done.11, f32[128,1024]{1,0:T(8,128)S(1)} %convolution_add_fusion, f32[1024]{0:T(1024)S(1)} %add_bitcast_fusion, f32[128]{0:T(128)S(1)} %copy-done.13), kind=kOutput, calls=%fused_computation.5 | convolution fusion | flops 203292672 | bytes 1118720 | tf_op jit(solution)/shard_map/dot_general | solution.py:131
  43.5 0.6 %convolution_bitcast_fusion.1 = f32[16,8,8,128]{3,1,2,0:T(8,128)S(1)} fusion(f32[128,128]{1,0:T(8,128)S(1)} %copy-done.11, f32[128,1024]{1,0:T(8,128)S(1)} %convolution_multiply_fusion), kind=kOutput, calls=%fused_computation.4 | convolution fusion | flops 201326592 | bytes 1114112 | tf_op jit(solution)/shard_map/dot_general | solution.py:140
  44.1 0.1 copy.22
  44.2 0.6 convolution_convert_fusion.1.x_ref
  44.8 13.2 %volume.1 = bf16[128,8,128]{2,1,0:T(8,128)(2,1)S(1)} custom-call(bf16[128,8,128]{2,1,0:T(8,128)(2,1)S(1)} %convolution_convert_fusion.1.x_ref), custom_call_target="tpu_custom_call" | custom-call | tf_op jit(solution)/shard_map/volume/pallas_call | solution.py:65
  58.0 2.4 %convolution_bitcast_fusion = f32[1,128,1024]{2,1,0:T(8,128)} fusion(f32[1024,1024]{1,0:T(8,128)S(1)} %copy-done.1, bf16[128,8,128]{2,1,0:T(8,128)(2,1)S(1)} %volume.1), kind=kOutput, calls=%fused_computation.3 | convolution fusion | flops 1610612736 | bytes 4980736 | tf_op jit(solution)/shard_map/dot_general | solution.py:143
  (46 shorter events, 0.3 us)
Async XLA Ops:
  0.0 0.9 %copy-start = (bf16[2,16,2048]{2,1,0:T(8,128)(2,1)S(1)}, bf16[2,16,2048]{2,1,0:T(8,128)(2,1)}, u32[]{:S(2)}) copy-start(bf16[2,16,2048]{2,1,0:T(8,128)(2,1)} %param.11) | copy-start | bytes 393220
  10.5 2.8 %copy-start.2 = (f32[8,128,1024]{2,1,0:T(8,128)S(1)}, f32[8,128,1024]{2,1,0:T(8,128)}, u32[]{:S(2)}) copy-start(f32[8,128,1024]{2,1,0:T(8,128)} %constant.153) | copy-start | bytes 12582916
  13.3 24.6 %copy-start.10 = (f32[128,1024]{1,0:T(8,128)S(1)}, f32[128,1024]{1,0:T(8,128)}, u32[]{:S(2)}) copy-start(f32[128,1024]{1,0:T(8,128)} %constant.154) | copy-start | bytes 1572868
  17.2 21.2 %copy-start.9 = (f32[128,1024]{1,0:T(8,128)S(1)}, f32[128,1024]{1,0:T(8,128)}, u32[]{:S(2)}) copy-start(f32[128,1024]{1,0:T(8,128)} %constant.155) | copy-start | bytes 1572868
  17.2 21.8 %copy-start.8 = (f32[128,1024]{1,0:T(8,128)S(1)}, f32[128,1024]{1,0:T(8,128)}, u32[]{:S(2)}) copy-start(f32[128,1024]{1,0:T(8,128)} %constant.156) | copy-start | bytes 1572868
  34.4 5.3 %copy-start.7 = (f32[128,1024]{1,0:T(8,128)S(1)}, f32[128,1024]{1,0:T(8,128)}, u32[]{:S(2)}) copy-start(f32[128,1024]{1,0:T(8,128)} %constant.157) | copy-start | bytes 1572868
  35.2 5.1 %copy-start.6 = (f32[128,1024]{1,0:T(8,128)S(1)}, f32[128,1024]{1,0:T(8,128)}, u32[]{:S(2)}) copy-start(f32[128,1024]{1,0:T(8,128)} %constant.158) | copy-start | bytes 1572868
  35.8 5.1 %copy-start.5 = (f32[128,1024]{1,0:T(8,128)S(1)}, f32[128,1024]{1,0:T(8,128)}, u32[]{:S(2)}) copy-start(f32[128,1024]{1,0:T(8,128)} %constant.159) | copy-start | bytes 1572868
  36.1 5.4 %copy-start.4 = (f32[128,1024]{1,0:T(8,128)S(1)}, f32[128,1024]{1,0:T(8,128)}, u32[]{:S(2)}) copy-start(f32[128,1024]{1,0:T(8,128)} %constant.160) | copy-start | bytes 1572868
  36.4 5.7 %copy-start.3 = (f32[128,1024]{1,0:T(8,128)S(1)}, f32[128,1024]{1,0:T(8,128)}, u32[]{:S(2)}) copy-start(f32[128,1024]{1,0:T(8,128)} %constant.161) | copy-start | bytes 1572868
  37.0 5.7 %copy-start.11 = (f32[128,128]{1,0:T(8,128)S(1)}, f32[128,128]{1,0:T(8,128)}, u32[]{:S(2)}) copy-start(f32[128,128]{1,0:T(8,128)} %constant.147.clone) | copy-start | bytes 196612
  37.0 5.7 %copy-start.13 = (f32[128]{0:T(128)S(1)}, f32[128]{0:T(128)}, u32[]{:S(2)}) copy-start(f32[128]{0:T(128)} %constant.148.clone) | copy-start | bytes 1540
  38.5 5.7 %copy-start.12 = (f32[128,128,1]{1,0,2:T(8,128)S(1)}, f32[128,128,1]{1,0,2:T(8,128)}, u32[]{:S(2)}) copy-start(f32[128,128,1]{1,0,2:T(8,128)} %constant.162) | copy-start | bytes 196612
  39.1 18.9 %copy-start.1 = (f32[1024,1024]{1,0:T(8,128)S(1)}, f32[1024,1024]{1,0:T(8,128)}, u32[]{:S(2)}) copy-start(f32[1024,1024]{1,0:T(8,128)} %constant.149.clone) | copy-start | bytes 12582916

commit v2 on v1

v2 whole, which is shorter than its diff:
```python
import math

import jax
import jax.numpy as jnp
import numpy as np
from jax import lax
from jax.experimental import pallas as pl
from jax.experimental.pallas import tpu as pltpu
from jax.sharding import PartitionSpec as P

NX, NU, NANG, NY, NZ = 1024, 2048, 1440, 128, 128
NP_DEV, YB, RB, HALO, BANDS, NPROJ = 2, 8, 16, 12, 16, 16
N = 128
KX = NX // N
ROWS = NP_DEV * RB
TILE = 256
WIN = 384
MESH = pl.DeviceIdType.MESH
lower_edge, upper_edge = 0.04, 0.35
f32, bf16 = jnp.float32, jnp.bfloat16


def real_basis(n):
    rows = np.arange(n)
    k = np.where(rows <= n // 2, rows, rows - n // 2)
    phase = 2.0 * np.pi * ((k[:, None] * rows[None, :]) % n) / n
    q = np.where((rows <= n // 2)[:, None], np.cos(phase), np.sin(phase))
    norm = np.where((rows == 0) | (rows == n // 2), 1.0 / n, 2.0 / n)
    return q * np.sqrt(norm)[:, None]


def ramp_tiles():
    n = np.arange(-(NU - 1), NU)
    odd = n % 2 != 0
    dist = np.where(odd, n, 1).astype(np.float32)
    values = np.where(n == 0, np.float32(0.25), np.where(odd, np.float32(-1.0) / (np.float32(math.pi * math.pi) * dist * dist), np.float32(0)))
    values = (values / np.float32(NX / NU)).astype(bf16)
    blocks = NU // TILE
    off = np.arange(1 - blocks, blocks)[:, None, None] * TILE
    at = off + np.arange(TILE)[None, :, None] - np.arange(TILE)[None, None, :]
    return values[at + NU - 1]


def tables():
    qx, qy, qz = real_basis(NX), real_basis(NY), real_basis(NZ)
    order = (np.arange(N)[None, :] * KX + np.arange(KX)[:, None]).reshape(-1)
    forward_x = qx.T[:, order]
    bands = np.zeros((YB, KX, BANDS, KX, NY))
    for k in range(KX):
        bands[:, k, :, k, :] = qy.reshape(NY, BANDS, YB).transpose(2, 1, 0)
    small = np.stack([qz, qz.T, qy])
    angle = (np.float32(2.0 * math.pi) * np.arange(NANG, dtype=np.float32) / np.float32(NANG)).astype(np.float64)
    trig = np.concatenate([np.cos(angle), np.sin(angle)]).astype(np.float32)
    return (
        jnp.asarray(ramp_tiles()),
        jnp.asarray(forward_x.astype(np.float32), bf16),
        jnp.asarray(bands.reshape(YB * KX * BANDS, KX * NY).astype(np.float32), bf16),
        jnp.asarray(qx.astype(np.float32), bf16),
        jnp.asarray(small.astype(np.float32), bf16),
        jnp.asarray(trig),
    )


def iota(shape, axis):
    return lax.broadcasted_iota(jnp.int32, shape, axis)


def dot(a, b):
    return jnp.dot(a, b, preferred_element_type=f32)


def fold_freq(row, n):
    k = jnp.where(row <= n // 2, row, row - n // 2).astype(f32) / n
    return k * k


def kernel(
    angle_ref, limit_ref, trig_ref, proj_ref,
    ramp_hbm, forward_hbm, bands_hbm, inverse_hbm, small_hbm,
    out_ref,
    ramp_ref, forward_ref, bands_ref, inverse_ref, small_ref,
    stack_ref, filt_ref, g_ref, send1, recv1, rows_ref, gain_ref, vol_ref, mix_ref, send2, recv2,
    table_sems, send_sems, recv_sems,
):
    d = lax.axis_index("depth")
    b = lax.axis_index("yband")
    me = d * BANDS + b

    def place(o):
        t = (me + o) & (N - 1)
        return t, (t >> 4, t & 15)

    loads = [
        pltpu.make_async_copy(src, dst, table_sems.at[i])
        for i, (src, dst) in enumerate(
            [(ramp_hbm, ramp_ref), (forward_hbm, forward_ref), (small_hbm, small_ref), (bands_hbm, bands_ref), (inverse_hbm, inverse_ref)]
        )
    ]
    for load in loads:
        load.start()

    bar = pltpu.get_barrier_semaphore()

    def greet(o, c):
        pl.semaphore_signal(bar, inc=1, device_id=place(o)[1], device_id_type=MESH)
        return c

    lax.fori_loop(1, N, greet, 0, unroll=True)

    blocks = NU // TILE
    for i in range(blocks):
        stack_ref[i * ROWS : (i + 1) * ROWS, :] = proj_ref[:, i * TILE : (i + 1) * TILE]
    loads[0].wait()
    acc = [jnp.zeros((ROWS, TILE), f32) for _ in range(blocks)]
    for k in range(1 - blocks, blocks):
        first, last = max(k, 0), blocks + min(k, 0)
        part = dot(stack_ref[first * ROWS : last * ROWS, :], ramp_ref[k + blocks - 1])
        for i in range(first, last):
            acc[i - k] += part[(i - first) * ROWS : (i - first + 1) * ROWS]
    for j in range(blocks):
        filt_ref[:, j * TILE : (j + 1) * TILE] = acc[j].astype(bf16)

    sub = iota((WIN, N), 0).astype(f32)
    lane_x = iota((1, N), 1).astype(f32)
    for p in range(NP_DEV):
        slope = jnp.full((1, N), 2.0 * trig_ref[angle_ref[d * NP_DEV + p]])
        rows = [filt_ref[p * RB : (p + 1) * RB, i * N : (i + 1) * N] for i in range(NU // N)]
        for i in range(NX // N):
            column = (NU - 1) / 2.0 + slope * ((lane_x + float(i * N)) - (NX - 1) / 2.0)
            ends = [(NU - 1) / 2.0 + slope * (i * N + end - (NX - 1) / 2.0) for end in (0.0, N - 1.0)]
            tile = jnp.clip(jnp.floor(jnp.minimum(ends[0], ends[1]) * (1.0 / N)), 0.0, float((NU - WIN) // N))
            column = column - tile * float(N)
            weights = jnp.maximum(0.0, 1.0 - jnp.abs(sub - column)).astype(bf16)
            window = rows
            for bit in (8, 4, 2, 1):
                up = tile >= float(bit)
                tile = jnp.where(up, tile - float(bit), tile)
                upper = jnp.broadcast_to(up, (RB, N))
                keep = bit - 1 + WIN // N
                window = [jnp.where(upper, window[k + bit], window[k]) if k + bit < len(window) else window[k] for k in range(keep)]
            g_ref[p * RB : (p + 1) * RB, i * N : (i + 1) * N] = dot(jnp.concatenate(window, axis=1), weights)

    g = g_ref[...]
    g_high = g.astype(bf16)
    g_low = (g - g_high.astype(f32)).astype(bf16)
    loads[1].wait()
    both = dot(jnp.concatenate([g_high, g_low], axis=0), forward_ref[...])
    spectrum = both[:ROWS] + both[ROWS:]
    for half in range(2):
        tall = jnp.concatenate([spectrum[:, k * N : (k + 1) * N] for k in range(4 * half, 4 * half + 4)], axis=0)
        send1[:, 0, half * N : (half + 1) * N] = tall.T
    lane = iota((N, N), 1)
    limits = jnp.where(lane < 64, limit_ref[0, 0], limit_ref[0, 1])
    send1[:, 0, 2 * N : 3 * N] = jnp.where((lane & 15) == b, limits, 0).astype(f32)

    def exchange(src, dst, s):
        def send(o, c):
            t, dev = place(o)
            pltpu.make_async_remote_copy(src.at[t], dst.at[me], send_sems.at[s], recv_sems.at[s], device_id=dev, device_id_type=MESH).start()
            return c

        lax.fori_loop(1, N, send, 0)
        dst[me] = src[me]

    def arrived(src, dst, s):
        view = dst.at[pl.ds(0, N - 1)]
        pltpu.make_async_copy(view, view, recv_sems.at[s]).wait()
        view = src.at[pl.ds(0, N - 1)]
        pltpu.make_async_copy(view, view, send_sems.at[s]).wait()

    pl.semaphore_wait(bar, N - 1)
    exchange(send1, recv1, 0)

    lanes = iota((1, 3 * 256), 1)
    proj = (lanes & 255) >> 4
    sines = jnp.zeros((1, 3 * 256), f32)
    for p in range(NPROJ):
        sines = jnp.where(proj == p, trig_ref[NANG + angle_ref[p]], sines)
    row_at = (16 * (lanes >> 8) - 16 + (lanes & 15)).astype(f32)
    tilt = (2.0 * iota((NZ, 1), 0).astype(f32) - (NZ - 1)) / (NZ - 1)
    away = row_at - (0.5 + (HALO - 1) * sines * tilt)
    for y in range(YB):
        rows_ref[y] = jnp.maximum(0.0, 1.0 - jnp.abs(away - 2.0 * y)).astype(bf16)
    fz = fold_freq(iota((NZ, 1), 0), NZ)
    fy = fold_freq(iota((1, NY), 1), NY)
    for k in range(KX):
        fx = fold_freq(me * KX + k + iota((1, NY), 1) * 0, NX)
        radius = fz + (fx + fy)
        low = (radius * (1.0 / (lower_edge * lower_edge))) ** 8
        up = (radius * (1.0 / (upper_edge * upper_edge))) ** 8
        gain_ref[:, k * NY : (k + 1) * NY] = low * (math.pi / NPROJ) / ((1.0 + low) * (1.0 + up))

    arrived(send1, recv1, 0)
    x = []
    for half in range(2):
        flat = recv1[:, 0, half * N : (half + 1) * N].T
        x += [flat[k * ROWS : (k + 1) * ROWS] for k in range(4)]
    group = iota((ROWS, N), 1) >> 4
    for bit in (1, 2, 4):
        clear = (group & bit) == 0
        for k in range(KX):
            if k & bit == 0:
                a, c = x[k], x[k + bit]
                x[k] = jnp.where(clear, a, pltpu.roll(c, 16 * bit, 1))
                x[k + bit] = jnp.where(clear, pltpu.roll(a, N - 16 * bit, 1), c)
    data = jnp.concatenate(x, axis=0)
    lims = jnp.sum(recv1[0:BANDS, 0, 2 * N : 3 * N], axis=0, keepdims=True)
    lane1 = iota((1, N), 1)
    swapped = pltpu.roll(lims, 64, 1)
    lo = jnp.where(lane1 < 64, lims, swapped)
    hi = jnp.where(lane1 < 64, swapped, lims)
    pieces = []
    for s in (-1, 0, 1):
        row = (16 * ((iota((RB, N), 1) & 15) + s) + iota((RB, N), 0)).astype(f32)
        ok = (row >= lo) & (row < hi) & (row >= 0.0) & (row < 256.0)
        keep = jnp.where(ok, 1.0, 0.0)
        moved = data if s == 0 else pltpu.roll(data, (-s) % N, 1)
        pieces += [(moved[r * RB : (r + 1) * RB] * keep).astype(bf16) for r in range(NPROJ)]
    extended = jnp.concatenate(pieces, axis=0)
    for y in range(YB):
        vol_ref[:, y * N : (y + 1) * N] = dot(rows_ref[y], extended).astype(bf16)
    loads[3].wait()
    loads[2].wait()
    along_y = dot(vol_ref[...], bands_ref[...]).astype(bf16)
    along_z = dot(small_ref[0], along_y) * gain_ref[...]
    back_z = dot(small_ref[1], along_z.astype(bf16)).astype(bf16)
    for k in range(KX):
        mix_ref[:, k, :] = dot(back_z[:, k * NY : (k + 1) * NY], small_ref[2])
    send2[...] = mix_ref[...].astype(bf16)
    exchange(send2, recv2, 1)
    arrived(send2, recv2, 1)
    loads[4].wait()
    tall = recv2[...].astype(f32).reshape(NX, NY)
    wide = jnp.concatenate([tall[i * N : (i + 1) * N].T for i in range(NX // N)], axis=1).astype(bf16)
    out_ref[0] = dot(wide, inverse_ref[...])


def on_device(projections, angle_index, row_ranges):
    ramp, forward, bands, inverse, small, trig = tables()
    smem = pl.BlockSpec(memory_space=pltpu.SMEM)
    vmem = pl.BlockSpec(memory_space=pltpu.VMEM)
    hbm = pl.BlockSpec(memory_space=pl.ANY)
    return pl.pallas_call(
        kernel,
        name="laminograph",
        out_shape=jax.ShapeDtypeStruct((1, NY, NX), f32),
        in_specs=[smem] * 3 + [vmem] + [hbm] * 5,
        out_specs=vmem,
        scratch_shapes=[
            pltpu.VMEM(ramp.shape, bf16),
            pltpu.VMEM(forward.shape, bf16),
            pltpu.VMEM(bands.shape, bf16),
            pltpu.VMEM(inverse.shape, bf16),
            pltpu.VMEM(small.shape, bf16),
            pltpu.VMEM((NU // TILE * ROWS, TILE), bf16),
            pltpu.VMEM((ROWS, NU), bf16),
            pltpu.VMEM((ROWS, NX), f32),
            pltpu.VMEM((N, 1, 3 * N), f32),
            pltpu.VMEM((N, 1, 3 * N), f32),
            pltpu.VMEM((YB, NZ, 3 * 256), bf16),
            pltpu.VMEM((NZ, KX * NY), f32),
            pltpu.VMEM((NZ, YB * N), bf16),
            pltpu.VMEM((NZ, KX, NY), f32),
            pltpu.VMEM((N, KX, NY), bf16),
            pltpu.VMEM((N, KX, NY), bf16),
            pltpu.SemaphoreType.DMA((5,)),
            pltpu.SemaphoreType.DMA((2,)),
            pltpu.SemaphoreType.DMA((2,)),
        ],
        compiler_params=pltpu.CompilerParams(collective_id=1, has_side_effects=True, vmem_limit_bytes=56 * 2**20),
    )(angle_index, row_ranges, trig, projections.reshape(ROWS, NU), ramp, forward, bands, inverse, small)


def solution(mesh):
    return jax.shard_map(
        on_device,
        mesh=mesh,
        in_specs=(P("depth", "yband", None), P(), P("yband", None)),
        out_specs=P(("depth", "yband"), None, None),
        check_vma=False,
    )
```

time: 60.6 us -> 30.8 us (0.51)
  matrix products: 22.9 us -> 0 us
  other arithmetic: 3.08 us -> 0 us
  local copies, waits for them, and re-layouts: 3.91 us -> 1.89 us
  Pallas kernels: 30 us -> 28.7 us
    dot_general x23 -> x0, matrix products: 22.9 us -> none  [the longest x1 4.93 us: on_device(): jnp.dot(projections.reshape(-1, NU), ramp, preferred_element_type=jnp.flo...]
    slice x5 -> x0, local copies, waits for them, and re-layouts: 1.39 us -> none  [the longest x1 1.28 us: on_device(): lim = jnp.where(lane < 64, row_ranges[0, 0], row_ranges[0, 1])]
    pallas_call x2 -> x1, Pallas kernels: 30 us -> 28.7 us  [on_device(): pl.pallas_call(kernel, name='laminograph', out_shape=jax.ShapeDtypeStruct...]
    convert_element_type x2 -> x0, other arithmetic: 1.2 us -> none  [the longest x1 1.19 us: on_device(): lim = jnp.where(lane % 16 == b, lim, 0).astype(jnp.float32)]
    add x2 -> x0, other arithmetic: 0.81 us -> none  [the longest x1 0.73 us: on_device(): rad = fz[:, None] + (fx[:, None] + fy[None, :]).reshape(1, 1024)]
    unnamed x30 -> x1, local copies, waits for them, and re-layouts: 1.1 us -> 1.89 us
    reshape x5 -> x0, local copies, waits for them, and re-layouts: 0.75 us -> none  [the longest x3 0.52 us: on_device(): r[:, :256].reshape(8, BANDS, KX, 32).transpose(0, 3, 2, 1).reshape(256, 128)]
    cos x1 -> x0, other arithmetic: 0.7 us -> none  [on_device(): cosines, sines = (jnp.cos(theta), jnp.sin(theta))]
where the time goes in v2:
time: 30.8 us; the launch traced here: 30.6 us
  Pallas kernels  28.7 us (93%)
  local copies, waits for them, and re-layouts  1.89 us (6%)
    pallas_call x1, Pallas kernels, on_device(): pl.pallas_call(kernel, name='laminograph', out_shape=jax.ShapeDtypeStruct...  28.7 us
    unnamed x1, local copies, waits for them, and re-layouts  1.89 us

profile of v2, /device:TPU:1, one launch (start us, length us, event | category | flops | bytes accessed | tf_op | source)
XLA Modules:
  0.0 30.6 jit_solution(7062307454547905088)
XLA Ops:
  0.0 28.7 %laminograph.1 = f32[1,128,1024]{2,1,0:T(8,128)} custom-call(s32[16]{0:T(128)} %angle_ref.1, s32[1,2]{1,0:T(1,128)} %limit_ref.1, f32[2880]{0:T(1024)} %constant.17.clone.trig_ref, bf16[32,2048]{1,0:T(8,128)(2,1)} %bitcast.1, bf16[15,256,256]{2,1,0:T(8,128)(2,1)} %constant.12.clone.ramp_hbm, bf16[1024,1024]{1,0:T(8,128)(2,1)} %constant.13.clone.forward_hbm, ...), custom_call_target="tpu_custom_call" | custom-call | tf_op jit(solution)/shard_map/laminograph/pallas_call | solution.py:243
  28.7 1.9 %copy.11 = f32[1,128,1024]{2,1,0:T(8,128)} copy(f32[1,128,1024]{2,1,0:T(8,128)} %laminograph.1) | data formatting | bytes 1048576

commit v3 on v2

--- a/solution.py
+++ b/solution.py
@@ -18,6 +18,15 @@
 MESH = pl.DeviceIdType.MESH
 lower_edge, upper_edge = 0.04, 0.35
 f32, bf16 = jnp.float32, jnp.bfloat16
+
+
+def far_first():
+    steps = [(x, y, z, c) for x in range(4) for y in range(4) for z in range(4) for c in range(2)]
+    hops = lambda s: sum(min(q, 4 - q) for q in s[:3])
+    return sorted(steps, key=lambda s: (-hops(s), s))[:-2] + [(0, 0, 0, 1)]
+
+
+STEPS = far_first()
 
 
 def real_basis(n):
@@ -76,24 +85,29 @@
 
 def kernel(
     angle_ref, limit_ref, trig_ref, proj_ref,
-    ramp_hbm, forward_hbm, bands_hbm, inverse_hbm, small_hbm,
-    out_ref,
-    ramp_ref, forward_ref, bands_ref, inverse_ref, small_ref,
-    stack_ref, filt_ref, g_ref, send1, recv1, rows_ref, gain_ref, vol_ref, mix_ref, send2, recv2,
+    ramp_hbm, forward_hbm, bands_hbm, small_hbm,
+    recv2,
+    ramp_ref, forward_ref, bands_ref, small_ref,
+    stack_ref, filt_ref, g_ref, send1, recv1, rows_ref, gain_ref, vol_ref, mix_ref, send2,
     table_sems, send_sems, recv_sems,
 ):
     d = lax.axis_index("depth")
     b = lax.axis_index("yband")
     me = d * BANDS + b
 
-    def place(o):
-        t = (me + o) & (N - 1)
-        return t, (t >> 4, t & 15)
+    px, py = ((d >> 2) << 1) | (b >> 3), d & 3
+    pz, pc = (b >> 1) & 3, b & 1
+
+    def place(step):
+        dx, dy, dz, dc = step
+        x, y, z, c = (px + dx) & 3, (py + dy) & 3, (pz + dz) & 3, pc ^ dc
+        dd, bb = ((x >> 1) << 2) | y, ((x & 1) << 3) | (z << 1) | c
+        return dd * BANDS + bb, (dd, bb)
 
     loads = [
         pltpu.make_async_copy(src, dst, table_sems.at[i])
         for i, (src, dst) in enumerate(
-            [(ramp_hbm, ramp_ref), (forward_hbm, forward_ref), (small_hbm, small_ref), (bands_hbm, bands_ref), (inverse_hbm, inverse_ref)]
+            [(ramp_hbm, ramp_ref), (forward_hbm, forward_ref), (small_hbm, small_ref), (bands_hbm, bands_ref)]
         )
     ]
     for load in loads:
@@ -101,11 +115,8 @@
 
     bar = pltpu.get_barrier_semaphore()
 
-    def greet(o, c):
-        pl.semaphore_signal(bar, inc=1, device_id=place(o)[1], device_id_type=MESH)
-        return c
-
-    lax.fori_loop(1, N, greet, 0, unroll=True)
+    for step in STEPS:
+        pl.semaphore_signal(bar, inc=1, device_id=place(step)[1], device_id_type=MESH)
 
     blocks = NU // TILE
     for i in range(blocks):
@@ -154,19 +165,14 @@
     send1[:, 0, 2 * N : 3 * N] = jnp.where((lane & 15) == b, limits, 0).astype(f32)
 
     def exchange(src, dst, s):
-        def send(o, c):
-            t, dev = place(o)
+        for step in STEPS:
+            t, dev = place(step)
             pltpu.make_async_remote_copy(src.at[t], dst.at[me], send_sems.at[s], recv_sems.at[s], device_id=dev, device_id_type=MESH).start()
-            return c
-
-        lax.fori_loop(1, N, send, 0)
         dst[me] = src[me]
 
     def arrived(src, dst, s):
         view = dst.at[pl.ds(0, N - 1)]
         pltpu.make_async_copy(view, view, recv_sems.at[s]).wait()
-        view = src.at[pl.ds(0, N - 1)]
-        pltpu.make_async_copy(view, view, send_sems.at[s]).wait()
 
     pl.semaphore_wait(bar, N - 1)
     exchange(send1, recv1, 0)
@@ -229,10 +235,9 @@
     send2[...] = mix_ref[...].astype(bf16)
     exchange(send2, recv2, 1)
     arrived(send2, recv2, 1)
-    loads[4].wait()
-    tall = recv2[...].astype(f32).reshape(NX, NY)
-    wide = jnp.concatenate([tall[i * N : (i + 1) * N].T for i in range(NX // N)], axis=1).astype(bf16)
-    out_ref[0] = dot(wide, inverse_ref[...])
+    for s, src in enumerate((send1, send2)):
+        view = src.at[pl.ds(0, N - 1)]
+        pltpu.make_async_copy(view, view, send_sems.at[s]).wait()
 
 
 def on_device(projections, angle_index, row_ranges):
@@ -240,17 +245,16 @@
     smem = pl.BlockSpec(memory_space=pltpu.SMEM)
     vmem = pl.BlockSpec(memory_space=pltpu.VMEM)
     hbm = pl.BlockSpec(memory_space=pl.ANY)
-    return pl.pallas_call(
+    back = pl.pallas_call(
         kernel,
         name="laminograph",
-        out_shape=jax.ShapeDtypeStruct((1, NY, NX), f32),
-        in_specs=[smem] * 3 + [vmem] + [hbm] * 5,
+        out_shape=jax.ShapeDtypeStruct((N, KX, NY), bf16),
+        in_specs=[smem] * 3 + [vmem] + [hbm] * 4,
         out_specs=vmem,
         scratch_shapes=[
             pltpu.VMEM(ramp.shape, bf16),
             pltpu.VMEM(forward.shape, bf16),
             pltpu.VMEM(bands.shape, bf16),
-            pltpu.VMEM(inverse.shape, bf16),
             pltpu.VMEM(small.shape, bf16),
             pltpu.VMEM((NU // TILE * ROWS, TILE), bf16),
             pltpu.VMEM((ROWS, NU), bf16),
@@ -262,13 +266,13 @@
             pltpu.VMEM((NZ, YB * N), bf16),
             pltpu.VMEM((NZ, KX, NY), f32),
             pltpu.VMEM((N, KX, NY), bf16),
-            pltpu.VMEM((N, KX, NY), bf16),
-            pltpu.SemaphoreType.DMA((5,)),
+            pltpu.SemaphoreType.DMA((4,)),
             pltpu.SemaphoreType.DMA((2,)),
             pltpu.SemaphoreType.DMA((2,)),
         ],
         compiler_params=pltpu.CompilerParams(collective_id=1, has_side_effects=True, vmem_limit_bytes=56 * 2**20),
-    )(angle_index, row_ranges, trig, projections.reshape(ROWS, NU), ramp, forward, bands, inverse, small)
+    )(angle_index, row_ranges, trig, projections.reshape(ROWS, NU), ramp, forward, bands, small)
+    return lax.dot_general(back.reshape(NX, NY), inverse, (((0,), (0,)), ((), ())), preferred_element_type=f32)[None]
 
 
 def solution(mesh):

time: 30.8 us -> 29.9 us (0.971)
  matrix products: 0 us -> 2.21 us
  local copies, waits for them, and re-layouts: 1.89 us -> 0.01 us
  Pallas kernels: 28.7 us -> 27.5 us
    dot_general x0 -> x1, matrix products: none -> 2.21 us  [on_device(): lax.dot_general(back.reshape(NX, NY), inverse, (((0,), (0,)), ((), ())),...]
    unnamed x1 -> x2, local copies, waits for them, and re-layouts: 1.89 us -> 0.01 us
    pallas_call x1, Pallas kernels: 28.7 us -> 27.5 us  [on_device(): pl.pallas_call(kernel, name='laminograph', out_shape=jax.ShapeDtypeStruct...]
where the time goes in v3:
time: 29.9 us; the launch traced here: 29.7 us
  Pallas kernels  27.5 us (92%)
  matrix products  2.21 us (7%)
    pallas_call x1, Pallas kernels, on_device(): pl.pallas_call(kernel, name='laminograph', out_shape=jax.ShapeDtypeStruct...  27.5 us
    dot_general x1, matrix products, on_device(): lax.dot_general(back.reshape(NX, NY), inverse, (((0,), (0,)), ((), ())),...  2.21 us

profile of v3, /device:TPU:1, one launch (start us, length us, event | category | flops | bytes accessed | tf_op | source)
XLA Modules:
  0.0 29.7 jit_solution(15510700682082557144)
XLA Ops:
  0.0 0.0 copy-start
  0.0 27.5 %laminograph.1 = bf16[128,8,128]{2,1,0:T(8,128)(2,1)} custom-call(s32[16]{0:T(128)} %angle_ref.1, s32[1,2]{1,0:T(1,128)} %limit_ref.1, f32[2880]{0:T(1024)} %constant.17.clone.trig_ref, bf16[32,2048]{1,0:T(8,128)(2,1)} %bitcast.7, bf16[15,256,256]{2,1,0:T(8,128)(2,1)} %constant.12.clone.ramp_hbm, bf16[1024,1024]{1,0:T(8,128)(2,1)} %constant.13.clone.forward_hbm, ...), custom_call_target="tpu_custom_call" | custom-call | tf_op jit(solution)/shard_map/laminograph/pallas_call | solution.py:248
  27.5 0.0 copy-done
  27.5 2.2 %convolution_bitcast_fusion = f32[1,128,1024]{2,1,0:T(8,128)} fusion(bf16[1024,1024]{1,0:T(8,128)(2,1)S(1)} %copy-done, bf16[128,8,128]{2,1,0:T(8,128)(2,1)} %laminograph.1), kind=kOutput, calls=%fused_computation | convolution fusion | flops 268435456 | bytes 2883584 | tf_op jit(solution)/shard_map/dot_general | solution.py:275
Async XLA Ops:
  0.0 27.5 %copy-start = (bf16[1024,1024]{1,0:T(8,128)(2,1)S(1)}, bf16[1024,1024]{1,0:T(8,128)(2,1)}, u32[]{:S(2)}) copy-start(bf16[1024,1024]{1,0:T(8,128)(2,1)} %constant.15.clone) | copy-start | bytes 6291460

commit v4 on v3

--- a/solution.py
+++ b/solution.py
@@ -26,7 +26,17 @@
     return sorted(steps, key=lambda s: (-hops(s), s))[:-2] + [(0, 0, 0, 1)]
 
 
+def far_chunks():
+    chunks = []
+    for high, y in sorted([(h, y) for h in range(2) for y in range(4)], key=lambda q: (-2 * q[0] - min(q[1], 4 - q[1]), q)):
+        inner = [(low, z, c) for low in range(2) for z in range(4) for c in range(2)]
+        inner.sort(key=lambda q: (-abs(2 * high - q[0]) - min(q[1], 4 - q[1]), q))
+        chunks.append([(high, low, y, z, c) for low, z, c in inner])
+    return chunks
+
+
 STEPS = far_first()
+CHUNKS = far_chunks()
 
 
 def real_basis(n):
@@ -84,11 +94,10 @@
 
 
 def kernel(
-    angle_ref, limit_ref, trig_ref, proj_ref,
-    ramp_hbm, forward_hbm, bands_hbm, small_hbm,
+    angle_hbm, limit_hbm, trig_hbm, proj_hbm, ramp_hbm, forward_hbm, bands_hbm, small_hbm,
     recv2,
-    ramp_ref, forward_ref, bands_ref, small_ref,
-    stack_ref, filt_ref, g_ref, send1, recv1, rows_ref, gain_ref, vol_ref, mix_ref, send2,
+    angle_ref, limit_ref, trig_ref, proj_ref, ramp_ref, forward_ref, bands_ref, small_ref,
+    stack_ref, filt_ref, g_ref, send1, recv1, rows_ref, gain_ref, vol_ref, back_ref, mix_ref, send2,
     table_sems, send_sems, recv_sems,
 ):
     d = lax.axis_index("depth")
@@ -104,24 +113,31 @@
         dd, bb = ((x >> 1) << 2) | y, ((x & 1) << 3) | (z << 1) | c
         return dd * BANDS + bb, (dd, bb)
 
-    loads = [
-        pltpu.make_async_copy(src, dst, table_sems.at[i])
-        for i, (src, dst) in enumerate(
-            [(ramp_hbm, ramp_ref), (forward_hbm, forward_ref), (small_hbm, small_ref), (bands_hbm, bands_ref)]
-        )
-    ]
-    for load in loads:
-        load.start()
+    def place2(step):
+        high, low, y, z, c = step
+        dd = (((d >> 2) ^ high) << 2) | ((py + y) & 3)
+        bb = (((b >> 3) ^ low) << 3) | (((pz + z) & 3) << 1) | (pc ^ c)
+        return dd * BANDS + bb, (dd, bb)
+
+    pairs = [(proj_hbm, proj_ref), (ramp_hbm, ramp_ref), (angle_hbm, angle_ref), (trig_hbm, trig_ref), (limit_hbm, limit_ref)]
+    pairs += [(forward_hbm, forward_ref), (small_hbm, small_ref), (bands_hbm, bands_ref)]
+    loads = [pltpu.make_async_copy(src, dst, table_sems.at[i]) for i, (src, dst) in enumerate(pairs)]
+    for i in (0, 1, 5):
+        loads[i].start()
 
     bar = pltpu.get_barrier_semaphore()
 
     for step in STEPS:
         pl.semaphore_signal(bar, inc=1, device_id=place(step)[1], device_id_type=MESH)
 
+    for i in (2, 3, 4, 6, 7):
+        loads[i].start()
+
     blocks = NU // TILE
+    loads[0].wait()
     for i in range(blocks):
         stack_ref[i * ROWS : (i + 1) * ROWS, :] = proj_ref[:, i * TILE : (i + 1) * TILE]
-    loads[0].wait()
+    loads[1].wait()
     acc = [jnp.zeros((ROWS, TILE), f32) for _ in range(blocks)]
     for k in range(1 - blocks, blocks):
         first, last = max(k, 0), blocks + min(k, 0)
@@ -131,6 +147,8 @@
     for j in range(blocks):
         filt_ref[:, j * TILE : (j + 1) * TILE] = acc[j].astype(bf16)
 
+    for load in loads[2:5]:
+        load.wait()
     sub = iota((WIN, N), 0).astype(f32)
     lane_x = iota((1, N), 1).astype(f32)
     for p in range(NP_DEV):
@@ -154,7 +172,7 @@
     g = g_ref[...]
     g_high = g.astype(bf16)
     g_low = (g - g_high.astype(f32)).astype(bf16)
-    loads[1].wait()
+    loads[5].wait()
     both = dot(jnp.concatenate([g_high, g_low], axis=0), forward_ref[...])
     spectrum = both[:ROWS] + both[ROWS:]
     for half in range(2):
@@ -225,15 +243,23 @@
     extended = jnp.concatenate(pieces, axis=0)
     for y in range(YB):
         vol_ref[:, y * N : (y + 1) * N] = dot(rows_ref[y], extended).astype(bf16)
-    loads[3].wait()
-    loads[2].wait()
+    loads[6].wait()
+    loads[7].wait()
     along_y = dot(vol_ref[...], bands_ref[...]).astype(bf16)
     along_z = dot(small_ref[0], along_y) * gain_ref[...]
-    back_z = dot(small_ref[1], along_z.astype(bf16)).astype(bf16)
-    for k in range(KX):
-        mix_ref[:, k, :] = dot(back_z[:, k * NY : (k + 1) * NY], small_ref[2])
-    send2[...] = mix_ref[...].astype(bf16)
-    exchange(send2, recv2, 1)
+    along_z = along_z.astype(bf16)
+    inverse_y = [dot(along_z[:, k * NY : (k + 1) * NY], small_ref[2]).astype(bf16) for k in range(KX)]
+    back_ref[...] = dot(small_ref[1], jnp.concatenate(inverse_y, axis=1))
+    for chunk in CHUNKS:
+        first = pl.multiple_of(place2(chunk[0])[1][0] * BANDS, BANDS)
+        for k in range(KX):
+            mix_ref[pl.ds(first, BANDS), k, :] = back_ref[pl.ds(first, BANDS), k * NY : (k + 1) * NY]
+        send2[pl.ds(first, BANDS)] = mix_ref[pl.ds(first, BANDS)].astype(bf16)
+        for step in chunk:
+            if any(step):
+                t, dev = place2(step)
+                pltpu.make_async_remote_copy(send2.at[t], recv2.at[me], send_sems.at[1], recv_sems.at[1], device_id=dev, device_id_type=MESH).start()
+    recv2[me] = send2[me]
     arrived(send2, recv2, 1)
     for s, src in enumerate((send1, send2)):
         view = src.at[pl.ds(0, N - 1)]
@@ -242,16 +268,19 @@
 
 def on_device(projections, angle_index, row_ranges):
     ramp, forward, bands, inverse, small, trig = tables()
-    smem = pl.BlockSpec(memory_space=pltpu.SMEM)
     vmem = pl.BlockSpec(memory_space=pltpu.VMEM)
     hbm = pl.BlockSpec(memory_space=pl.ANY)
     back = pl.pallas_call(
         kernel,
         name="laminograph",
         out_shape=jax.ShapeDtypeStruct((N, KX, NY), bf16),
-        in_specs=[smem] * 3 + [vmem] + [hbm] * 4,
+        in_specs=[hbm] * 8,
         out_specs=vmem,
         scratch_shapes=[
+            pltpu.SMEM((NPROJ,), jnp.int32),
+            pltpu.SMEM((1, 2), jnp.int32),
+            pltpu.SMEM(trig.shape, f32),
+            pltpu.VMEM((ROWS, NU), bf16),
             pltpu.VMEM(ramp.shape, bf16),
             pltpu.VMEM(forward.shape, bf16),
             pltpu.VMEM(bands.shape, bf16),
@@ -264,9 +293,10 @@
             pltpu.VMEM((YB, NZ, 3 * 256), bf16),
             pltpu.VMEM((NZ, KX * NY), f32),
             pltpu.VMEM((NZ, YB * N), bf16),
+            pltpu.VMEM((NZ, KX * NY), f32),
             pltpu.VMEM((NZ, KX, NY), f32),
             pltpu.VMEM((N, KX, NY), bf16),
-            pltpu.SemaphoreType.DMA((4,)),
+            pltpu.SemaphoreType.DMA((8,)),
             pltpu.SemaphoreType.DMA((2,)),
             pltpu.SemaphoreType.DMA((2,)),
         ],

time: 29.9 us -> 28.4 us (0.950)
  Pallas kernels: 27.5 us -> 26.1 us
    pallas_call x1, Pallas kernels: 27.5 us -> 26.1 us  [on_device(): pl.pallas_call(kernel, name='laminograph', out_shape=jax.ShapeDtypeStruct...]
where the time goes in v4:
time: 28.4 us; the launch traced here: 28.3 us
  Pallas kernels  26.1 us (92%)
  matrix products  2.22 us (8%)
    pallas_call x1, Pallas kernels, on_device(): pl.pallas_call(kernel, name='laminograph', out_shape=jax.ShapeDtypeStruct...  26.1 us
    dot_general x1, matrix products, on_device(): lax.dot_general(back.reshape(NX, NY), inverse, (((0,), (0,)), ((), ())),...  2.22 us

profile of v4, /device:TPU:1, one launch (start us, length us, event | category | flops | bytes accessed | tf_op | source)
XLA Modules:
  0.0 28.3 jit_solution(15814326593944903502)
XLA Ops:
  0.0 0.0 copy-start
  0.0 26.1 %laminograph.1 = bf16[128,8,128]{2,1,0:T(8,128)(2,1)} custom-call(s32[16]{0:T(128)} %angle_hbm.1, s32[1,2]{1,0:T(1,128)} %limit_hbm.1, f32[2880]{0:T(1024)} %constant.17.clone.trig_hbm, bf16[32,2048]{1,0:T(8,128)(2,1)} %bitcast.7, bf16[15,256,256]{2,1,0:T(8,128)(2,1)} %constant.12.clone.ramp_hbm, bf16[1024,1024]{1,0:T(8,128)(2,1)} %constant.13.clone.forward_hbm, ...), custom_call_target="tpu_custom_call" | custom-call | tf_op jit(solution)/shard_map/laminograph/pallas_call | solution.py:273
  26.1 0.0 copy-done
  26.1 2.2 %convolution_bitcast_fusion = f32[1,128,1024]{2,1,0:T(8,128)} fusion(bf16[1024,1024]{1,0:T(8,128)(2,1)S(1)} %copy-done, bf16[128,8,128]{2,1,0:T(8,128)(2,1)} %laminograph.1), kind=kOutput, calls=%fused_computation | convolution fusion | flops 268435456 | bytes 2883584 | tf_op jit(solution)/shard_map/dot_general | solution.py:305
Async XLA Ops:
  0.0 26.1 %copy-start = (bf16[1024,1024]{1,0:T(8,128)(2,1)S(1)}, bf16[1024,1024]{1,0:T(8,128)(2,1)}, u32[]{:S(2)}) copy-start(bf16[1024,1024]{1,0:T(8,128)(2,1)} %constant.15.clone) | copy-start | bytes 6291460

commit v5 on v4

--- a/solution.py
+++ b/solution.py
@@ -64,16 +64,13 @@
     qx, qy, qz = real_basis(NX), real_basis(NY), real_basis(NZ)
     order = (np.arange(N)[None, :] * KX + np.arange(KX)[:, None]).reshape(-1)
     forward_x = qx.T[:, order]
-    bands = np.zeros((YB, KX, BANDS, KX, NY))
-    for k in range(KX):
-        bands[:, k, :, k, :] = qy.reshape(NY, BANDS, YB).transpose(2, 1, 0)
-    small = np.stack([qz, qz.T, qy])
+    by_band = qy.reshape(NY, BANDS, YB).transpose(0, 2, 1).reshape(NY, NY)
+    small = np.stack([qz.T, by_band, qy.T])
     angle = (np.float32(2.0 * math.pi) * np.arange(NANG, dtype=np.float32) / np.float32(NANG)).astype(np.float64)
     trig = np.concatenate([np.cos(angle), np.sin(angle)]).astype(np.float32)
     return (
         jnp.asarray(ramp_tiles()),
         jnp.asarray(forward_x.astype(np.float32), bf16),
-        jnp.asarray(bands.reshape(YB * KX * BANDS, KX * NY).astype(np.float32), bf16),
         jnp.asarray(qx.astype(np.float32), bf16),
         jnp.asarray(small.astype(np.float32), bf16),
         jnp.asarray(trig),
@@ -94,10 +91,10 @@
 
 
 def kernel(
-    angle_hbm, limit_hbm, trig_hbm, proj_hbm, ramp_hbm, forward_hbm, bands_hbm, small_hbm,
+    angle_hbm, limit_hbm, trig_hbm, proj_hbm, ramp_hbm, forward_hbm, small_hbm,
     recv2,
-    angle_ref, limit_ref, trig_ref, proj_ref, ramp_ref, forward_ref, bands_ref, small_ref,
-    stack_ref, filt_ref, g_ref, send1, recv1, rows_ref, gain_ref, vol_ref, back_ref, mix_ref, send2,
+    angle_ref, limit_ref, trig_ref, proj_ref, ramp_ref, forward_ref, small_ref,
+    stack_ref, filt_ref, g_ref, send1, recv1, rows_ref, gain_ref, back_ref, mix_ref, send2,
     table_sems, send_sems, recv_sems,
 ):
     d = lax.axis_index("depth")
@@ -120,7 +117,7 @@
         return dd * BANDS + bb, (dd, bb)
 
     pairs = [(proj_hbm, proj_ref), (ramp_hbm, ramp_ref), (angle_hbm, angle_ref), (trig_hbm, trig_ref), (limit_hbm, limit_ref)]
-    pairs += [(forward_hbm, forward_ref), (small_hbm, small_ref), (bands_hbm, bands_ref)]
+    pairs += [(forward_hbm, forward_ref), (small_hbm, small_ref)]
     loads = [pltpu.make_async_copy(src, dst, table_sems.at[i]) for i, (src, dst) in enumerate(pairs)]
     for i in (0, 1, 5):
         loads[i].start()
@@ -130,7 +127,7 @@
     for step in STEPS:
         pl.semaphore_signal(bar, inc=1, device_id=place(step)[1], device_id_type=MESH)
 
-    for i in (2, 3, 4, 6, 7):
+    for i in (2, 3, 4, 6):
         loads[i].start()
 
     blocks = NU // TILE
@@ -180,7 +177,7 @@
         send1[:, 0, half * N : (half + 1) * N] = tall.T
     lane = iota((N, N), 1)
     limits = jnp.where(lane < 64, limit_ref[0, 0], limit_ref[0, 1])
-    send1[:, 0, 2 * N : 3 * N] = jnp.where((lane & 15) == b, limits, 0).astype(f32)
+    send1[:, 0, 2 * N : 3 * N] = limits.astype(f32)
 
     def exchange(src, dst, s):
         for step in STEPS:
@@ -195,61 +192,61 @@
     pl.semaphore_wait(bar, N - 1)
     exchange(send1, recv1, 0)
 
-    lanes = iota((1, 3 * 256), 1)
-    proj = (lanes & 255) >> 4
-    sines = jnp.zeros((1, 3 * 256), f32)
-    for p in range(NPROJ):
-        sines = jnp.where(proj == p, trig_ref[NANG + angle_ref[p]], sines)
-    row_at = (16 * (lanes >> 8) - 16 + (lanes & 15)).astype(f32)
-    tilt = (2.0 * iota((NZ, 1), 0).astype(f32) - (NZ - 1)) / (NZ - 1)
-    away = row_at - (0.5 + (HALO - 1) * sines * tilt)
+    loads[6].wait()
+    detector = iota((RB, NZ), 0).astype(f32)
+    tilt = (2.0 * iota((1, NZ), 1).astype(f32) - (NZ - 1)) / (NZ - 1)
+    offsets = [0.5 + (HALO - 1) * trig_ref[NANG + angle_ref[p]] * tilt for p in range(NPROJ)]
+    away = jnp.concatenate([detector + 16.0 * s - offsets[p] for s in (-1, 0, 1) for p in range(NPROJ)], axis=0)
     for y in range(YB):
-        rows_ref[y] = jnp.maximum(0.0, 1.0 - jnp.abs(away - 2.0 * y)).astype(bf16)
-    fz = fold_freq(iota((NZ, 1), 0), NZ)
-    fy = fold_freq(iota((1, NY), 1), NY)
+        weights = jnp.maximum(0.0, 1.0 - jnp.abs(away - 2.0 * y)).astype(bf16)
+        rows_ref[:, y * NZ : (y + 1) * NZ] = dot(weights, small_ref[0]).astype(bf16)
+    fy = fold_freq(iota((NY, 1), 0), NY)
+    fz = fold_freq(iota((1, NZ), 1), NZ)
     for k in range(KX):
-        fx = fold_freq(me * KX + k + iota((1, NY), 1) * 0, NX)
-        radius = fz + (fx + fy)
+        fx = fold_freq(me * KX + k + iota((1, NZ), 1) * 0, NX)
+        radius = fy + (fx + fz)
         low = (radius * (1.0 / (lower_edge * lower_edge))) ** 8
         up = (radius * (1.0 / (upper_edge * upper_edge))) ** 8
-        gain_ref[:, k * NY : (k + 1) * NY] = low * (math.pi / NPROJ) / ((1.0 + low) * (1.0 + up))
+        gain_ref[:, k * NZ : (k + 1) * NZ] = low * (math.pi / NPROJ) / ((1.0 + low) * (1.0 + up))
 
     arrived(send1, recv1, 0)
-    x = []
+    group = iota((BANDS, N), 1) >> 5
+    field = [[None, None] for _ in range(KX)]
     for half in range(2):
-        flat = recv1[:, 0, half * N : (half + 1) * N].T
-        x += [flat[k * ROWS : (k + 1) * ROWS] for k in range(4)]
-    group = iota((ROWS, N), 1) >> 4
-    for bit in (1, 2, 4):
-        clear = (group & bit) == 0
-        for k in range(KX):
-            if k & bit == 0:
-                a, c = x[k], x[k + bit]
-                x[k] = jnp.where(clear, a, pltpu.roll(c, 16 * bit, 1))
-                x[k + bit] = jnp.where(clear, pltpu.roll(a, N - 16 * bit, 1), c)
-    data = jnp.concatenate(x, axis=0)
-    lims = jnp.sum(recv1[0:BANDS, 0, 2 * N : 3 * N], axis=0, keepdims=True)
-    lane1 = iota((1, N), 1)
+        for j in range(2):
+            x = [recv1[(4 * j + q) * BANDS : (4 * j + q + 1) * BANDS, 0, half * N : (half + 1) * N] for q in range(4)]
+            for bit in (1, 2):
+                clear = (group & bit) == 0
+                for q in range(4):
+                    if q & bit == 0:
+                        a, c = x[q], x[q + bit]
+                        x[q] = jnp.where(clear, a, pltpu.roll(c, 32 * bit, 1))
+                        x[q + bit] = jnp.where(clear, pltpu.roll(a, N - 32 * bit, 1), c)
+            for q in range(4):
+                field[4 * half + q][j] = x[q]
+    lims = recv1[0:BANDS, 0, 2 * N : 3 * N]
     swapped = pltpu.roll(lims, 64, 1)
-    lo = jnp.where(lane1 < 64, lims, swapped)
-    hi = jnp.where(lane1 < 64, swapped, lims)
-    pieces = []
+    left = iota((BANDS, N), 1) < 64
+    lo, hi = jnp.where(left, lims, swapped), jnp.where(left, swapped, lims)
+    columns = []
     for s in (-1, 0, 1):
-        row = (16 * ((iota((RB, N), 1) & 15) + s) + iota((RB, N), 0)).astype(f32)
+        row = (16 * (iota((BANDS, N), 0) + s) + (iota((BANDS, N), 1) & 15)).astype(f32)
         ok = (row >= lo) & (row < hi) & (row >= 0.0) & (row < 256.0)
         keep = jnp.where(ok, 1.0, 0.0)
-        moved = data if s == 0 else pltpu.roll(data, (-s) % N, 1)
-        pieces += [(moved[r * RB : (r + 1) * RB] * keep).astype(bf16) for r in range(NPROJ)]
-    extended = jnp.concatenate(pieces, axis=0)
-    for y in range(YB):
-        vol_ref[:, y * N : (y + 1) * N] = dot(rows_ref[y], extended).astype(bf16)
-    loads[6].wait()
-    loads[7].wait()
-    along_y = dot(vol_ref[...], bands_ref[...]).astype(bf16)
-    along_z = dot(small_ref[0], along_y) * gain_ref[...]
-    along_z = along_z.astype(bf16)
-    inverse_y = [dot(along_z[:, k * NY : (k + 1) * NY], small_ref[2]).astype(bf16) for k in range(KX)]
-    back_ref[...] = dot(small_ref[1], jnp.concatenate(inverse_y, axis=1))
+        for j in range(2):
+            moved = [field[k][j] if s == 0 else pltpu.roll(field[k][j], (-s) % BANDS, 0) for k in range(KX)]
+            columns.append(jnp.concatenate([(m * keep).astype(bf16) for m in moved], axis=0))
+    vol = dot(jnp.concatenate(columns, axis=1), rows_ref[...]).astype(bf16)
+    tall = [
+        jnp.concatenate([vol[k * BANDS : (k + 1) * BANDS, y * NZ : (y + 1) * NZ] for y in range(YB)], axis=0)
+        for k in range(KX)
+    ]
+    along_y = dot(small_ref[1], jnp.concatenate(tall, axis=1))
+    back_y = dot(small_ref[2], (along_y * gain_ref[...]).astype(bf16)).astype(bf16)
+    for k in range(KX):
+        back_ref[:, k * NY : (k + 1) * NY] = lax.dot_general(
+            small_ref[0], back_y[:, k * NZ : (k + 1) * NZ], (((1,), (1,)), ((), ())), preferred_element_type=f32
+        )
     for chunk in CHUNKS:
         first = pl.multiple_of(place2(chunk[0])[1][0] * BANDS, BANDS)
         for k in range(KX):
@@ -267,14 +264,14 @@
 
 
 def on_device(projections, angle_index, row_ranges):
-    ramp, forward, bands, inverse, small, trig = tables()
+    ramp, forward, inverse, small, trig = tables()
     vmem = pl.BlockSpec(memory_space=pltpu.VMEM)
     hbm = pl.BlockSpec(memory_space=pl.ANY)
     back = pl.pallas_call(
         kernel,
         name="laminograph",
         out_shape=jax.ShapeDtypeStruct((N, KX, NY), bf16),
-        in_specs=[hbm] * 8,
+        in_specs=[hbm] * 7,
         out_specs=vmem,
         scratch_shapes=[
             pltpu.SMEM((NPROJ,), jnp.int32),
@@ -283,25 +280,23 @@
             pltpu.VMEM((ROWS, NU), bf16),
             pltpu.VMEM(ramp.shape, bf16),
             pltpu.VMEM(forward.shape, bf16),
-            pltpu.VMEM(bands.shape, bf16),
             pltpu.VMEM(small.shape, bf16),
             pltpu.VMEM((NU // TILE * ROWS, TILE), bf16),
             pltpu.VMEM((ROWS, NU), bf16),
             pltpu.VMEM((ROWS, NX), f32),
             pltpu.VMEM((N, 1, 3 * N), f32),
             pltpu.VMEM((N, 1, 3 * N), f32),
-            pltpu.VMEM((YB, NZ, 3 * 256), bf16),
+            pltpu.VMEM((3 * 256, YB * NZ), bf16),
             pltpu.VMEM((NZ, KX * NY), f32),
-            pltpu.VMEM((NZ, YB * N), bf16),
             pltpu.VMEM((NZ, KX * NY), f32),
             pltpu.VMEM((NZ, KX, NY), f32),
             pltpu.VMEM((N, KX, NY), bf16),
-            pltpu.SemaphoreType.DMA((8,)),
+            pltpu.SemaphoreType.DMA((7,)),
             pltpu.SemaphoreType.DMA((2,)),
             pltpu.SemaphoreType.DMA((2,)),
         ],
         compiler_params=pltpu.CompilerParams(collective_id=1, has_side_effects=True, vmem_limit_bytes=56 * 2**20),
-    )(angle_index, row_ranges, trig, projections.reshape(ROWS, NU), ramp, forward, bands, small)
+    )(angle_index, row_ranges, trig, projections.reshape(ROWS, NU), ramp, forward, small)
     return lax.dot_general(back.reshape(NX, NY), inverse, (((0,), (0,)), ((), ())), preferred_element_type=f32)[None]
 
 

time: 28.4 us -> 27.6 us (0.972)
  Pallas kernels: 26.1 us -> 25.2 us
    pallas_call x1, Pallas kernels: 26.1 us -> 25.2 us  [on_device(): pl.pallas_call(kernel, name='laminograph', out_shape=jax.ShapeDtypeStruct...]
where the time goes in v5:
time: 27.6 us; the launch traced here: 27.4 us
  Pallas kernels  25.2 us (91%)
  matrix products  2.21 us (8%)
    pallas_call x1, Pallas kernels, on_device(): pl.pallas_call(kernel, name='laminograph', out_shape=jax.ShapeDtypeStruct...  25.2 us
    dot_general x1, matrix products, on_device(): lax.dot_general(back.reshape(NX, NY), inverse, (((0,), (0,)), ((), ())),...  2.21 us

profile of v5, /device:TPU:1, one launch (start us, length us, event | category | flops | bytes accessed | tf_op | source)
XLA Modules:
  0.0 27.4 jit_solution(11224246820590875935)
XLA Ops:
  0.0 0.0 copy-start
  0.0 25.2 %laminograph.1 = bf16[128,8,128]{2,1,0:T(8,128)(2,1)} custom-call(s32[16]{0:T(128)} %angle_hbm.1, s32[1,2]{1,0:T(1,128)} %limit_hbm.1, f32[2880]{0:T(1024)} %constant.14.clone.trig_hbm, bf16[32,2048]{1,0:T(8,128)(2,1)} %bitcast.7, bf16[15,256,256]{2,1,0:T(8,128)(2,1)} %constant.10.clone.ramp_hbm, bf16[1024,1024]{1,0:T(8,128)(2,1)} %constant.11.clone.forward_hbm, ...), custom_call_target="tpu_custom_call" | custom-call | tf_op jit(solution)/shard_map/laminograph/pallas_call | solution.py:270
  25.2 0.0 copy-done
  25.2 2.2 %convolution_bitcast_fusion = f32[1,128,1024]{2,1,0:T(8,128)} fusion(bf16[1024,1024]{1,0:T(8,128)(2,1)S(1)} %copy-done, bf16[128,8,128]{2,1,0:T(8,128)(2,1)} %laminograph.1), kind=kOutput, calls=%fused_computation | convolution fusion | flops 268435456 | bytes 2883584 | tf_op jit(solution)/shard_map/dot_general | solution.py:300
Async XLA Ops:
  0.0 25.2 %copy-start = (bf16[1024,1024]{1,0:T(8,128)(2,1)S(1)}, bf16[1024,1024]{1,0:T(8,128)(2,1)}, u32[]{:S(2)}) copy-start(bf16[1024,1024]{1,0:T(8,128)(2,1)} %constant.12.clone) | copy-start | bytes 6291460

commit v6 on v5

--- a/solution.py
+++ b/solution.py
@@ -295,8 +295,8 @@
             pltpu.SemaphoreType.DMA((2,)),
             pltpu.SemaphoreType.DMA((2,)),
         ],
-        compiler_params=pltpu.CompilerParams(collective_id=1, has_side_effects=True, vmem_limit_bytes=56 * 2**20),
-    )(angle_index, row_ranges, trig, projections.reshape(ROWS, NU), ramp, forward, small)
+        compiler_params=pltpu.CompilerParams(collective_id=1, has_side_effects=True, vmem_limit_bytes=24 * 2**20),
+    )(*[pltpu.with_memory_space_constraint(x, pltpu.HBM) for x in (angle_index, row_ranges, trig, projections.reshape(ROWS, NU), ramp, forward, small)])
     return lax.dot_general(back.reshape(NX, NY), inverse, (((0,), (0,)), ((), ())), preferred_element_type=f32)[None]
 
 

time: 27.6 us -> 25.9 us (0.938)
  matrix products: 2.21 us -> 1.27 us
  Pallas kernels: 25.2 us -> 24.5 us
    dot_general x1, matrix products: 2.21 us -> 1.27 us  [on_device(): lax.dot_general(back.reshape(NX, NY), inverse, (((0,), (0,)), ((), ())),...]
    pallas_call x1, Pallas kernels: 25.2 us -> 24.5 us  [on_device(): pl.pallas_call(kernel, name='laminograph', out_shape=jax.ShapeDtypeStruct...]
where the time goes in v6:
time: 25.9 us; the launch traced here: 25.8 us
  Pallas kernels  24.5 us (95%)
  matrix products  1.27 us (5%)
    pallas_call x1, Pallas kernels, on_device(): pl.pallas_call(kernel, name='laminograph', out_shape=jax.ShapeDtypeStruct...  24.5 us
    dot_general x1, matrix products, on_device(): lax.dot_general(back.reshape(NX, NY), inverse, (((0,), (0,)), ((), ())),...  1.27 us

profile of v6, /device:TPU:1, one launch (start us, length us, event | category | flops | bytes accessed | tf_op | source)
XLA Modules:
  0.0 25.8 jit_solution(8320948703939751179)
XLA Ops:
  0.0 0.0 copy-start
  0.0 24.5 %laminograph.1 = bf16[128,8,128]{2,1,0:T(8,128)(2,1)S(1)} custom-call(s32[16]{0:T(128)} %angle_hbm.1, s32[1,2]{1,0:T(1,128)} %limit_hbm.1, f32[2880]{0:T(1024)} %constant.14.clone.trig_hbm, bf16[32,2048]{1,0:T(8,128)(2,1)} %bitcast.7, bf16[15,256,256]{2,1,0:T(8,128)(2,1)} %constant.10.clone.ramp_hbm, bf16[1024,1024]{1,0:T(8,128)(2,1)} %constant.11.clone.forward_hbm, ...), custom_call_target="tpu_custom_call" | custom-call | tf_op jit(solution)/shard_map/laminograph/pallas_call | solution.py:270
  24.5 0.0 copy-done
  24.5 1.3 %convolution_bitcast_fusion = f32[1,128,1024]{2,1,0:T(8,128)} fusion(bf16[1024,1024]{1,0:T(8,128)(2,1)S(1)} %copy-done, bf16[128,8,128]{2,1,0:T(8,128)(2,1)S(1)} %laminograph.1), kind=kOutput, calls=%fused_computation | convolution fusion | flops 268435456 | bytes 2883584 | tf_op jit(solution)/shard_map/dot_general | solution.py:300
Async XLA Ops:
  0.0 24.5 %copy-start = (bf16[1024,1024]{1,0:T(8,128)(2,1)S(1)}, bf16[1024,1024]{1,0:T(8,128)(2,1)}, u32[]{:S(2)}) copy-start(bf16[1024,1024]{1,0:T(8,128)(2,1)} %constant.12.clone) | copy-start | bytes 6291460

commit v7 on v6

--- a/solution.py
+++ b/solution.py
@@ -95,7 +95,7 @@
     recv2,
     angle_ref, limit_ref, trig_ref, proj_ref, ramp_ref, forward_ref, small_ref,
     stack_ref, filt_ref, g_ref, send1, recv1, rows_ref, gain_ref, back_ref, mix_ref, send2,
-    table_sems, send_sems, recv_sems,
+    limit_out, limit_in, table_sems, send_sems, recv_sems, limit_sems,
 ):
     d = lax.axis_index("depth")
     b = lax.axis_index("yband")
@@ -177,7 +177,7 @@
         send1[:, 0, half * N : (half + 1) * N] = tall.T
     lane = iota((N, N), 1)
     limits = jnp.where(lane < 64, limit_ref[0, 0], limit_ref[0, 1])
-    send1[:, 0, 2 * N : 3 * N] = limits.astype(f32)
+    limit_out[0] = limits[0:1].astype(f32)
 
     def exchange(src, dst, s):
         for step in STEPS:
@@ -191,6 +191,11 @@
 
     pl.semaphore_wait(bar, N - 1)
     exchange(send1, recv1, 0)
+    for o in range(1, BANDS):
+        pltpu.make_async_remote_copy(
+            limit_out.at[0], limit_in.at[b], limit_sems.at[0], limit_sems.at[1], device_id=(d, (b + o) & 15), device_id_type=MESH
+        ).start()
+    limit_in[b] = limit_out[0]
 
     loads[6].wait()
     detector = iota((RB, NZ), 0).astype(f32)
@@ -224,7 +229,9 @@
                         x[q + bit] = jnp.where(clear, pltpu.roll(a, N - 32 * bit, 1), c)
             for q in range(4):
                 field[4 * half + q][j] = x[q]
-    lims = recv1[0:BANDS, 0, 2 * N : 3 * N]
+    landed = limit_in.at[pl.ds(0, BANDS - 1)]
+    pltpu.make_async_copy(landed, landed, limit_sems.at[1]).wait()
+    lims = limit_in[:, 0, :]
     swapped = pltpu.roll(lims, 64, 1)
     left = iota((BANDS, N), 1) < 64
     lo, hi = jnp.where(left, lims, swapped), jnp.where(left, swapped, lims)
@@ -258,6 +265,7 @@
                 pltpu.make_async_remote_copy(send2.at[t], recv2.at[me], send_sems.at[1], recv_sems.at[1], device_id=dev, device_id_type=MESH).start()
     recv2[me] = send2[me]
     arrived(send2, recv2, 1)
+    pltpu.make_async_copy(landed, landed, limit_sems.at[0]).wait()
     for s, src in enumerate((send1, send2)):
         view = src.at[pl.ds(0, N - 1)]
         pltpu.make_async_copy(view, view, send_sems.at[s]).wait()
@@ -284,14 +292,17 @@
             pltpu.VMEM((NU // TILE * ROWS, TILE), bf16),
             pltpu.VMEM((ROWS, NU), bf16),
             pltpu.VMEM((ROWS, NX), f32),
-            pltpu.VMEM((N, 1, 3 * N), f32),
-            pltpu.VMEM((N, 1, 3 * N), f32),
+            pltpu.VMEM((N, 1, 2 * N), f32),
+            pltpu.VMEM((N, 1, 2 * N), f32),
             pltpu.VMEM((3 * 256, YB * NZ), bf16),
             pltpu.VMEM((NZ, KX * NY), f32),
             pltpu.VMEM((NZ, KX * NY), f32),
             pltpu.VMEM((NZ, KX, NY), f32),
             pltpu.VMEM((N, KX, NY), bf16),
+            pltpu.VMEM((1, 1, N), f32),
+            pltpu.VMEM((BANDS, 1, N), f32),
             pltpu.SemaphoreType.DMA((7,)),
+            pltpu.SemaphoreType.DMA((2,)),
             pltpu.SemaphoreType.DMA((2,)),
             pltpu.SemaphoreType.DMA((2,)),
         ],

time: 25.9 us -> 25.6 us (0.988)
  Pallas kernels: 24.5 us -> 24.2 us
    pallas_call x1, Pallas kernels: 24.5 us -> 24.2 us  [on_device(): pl.pallas_call(kernel, name='laminograph', out_shape=jax.ShapeDtypeStruct...]
where the time goes in v7:
time: 25.6 us; the launch traced here: 25.5 us
  Pallas kernels  24.2 us (95%)
  matrix products  1.26 us (5%)
    pallas_call x1, Pallas kernels, on_device(): pl.pallas_call(kernel, name='laminograph', out_shape=jax.ShapeDtypeStruct...  24.2 us
    dot_general x1, matrix products, on_device(): lax.dot_general(back.reshape(NX, NY), inverse, (((0,), (0,)), ((), ())),...  1.26 us

profile of v7, /device:TPU:1, one launch (start us, length us, event | category | flops | bytes accessed | tf_op | source)
XLA Modules:
  0.0 25.5 jit_solution(14003748488441788377)
XLA Ops:
  0.0 0.0 copy-start
  0.0 24.2 %laminograph.1 = bf16[128,8,128]{2,1,0:T(8,128)(2,1)S(1)} custom-call(s32[16]{0:T(128)} %angle_hbm.1, s32[1,2]{1,0:T(1,128)} %limit_hbm.1, f32[2880]{0:T(1024)} %constant.14.clone.trig_hbm, bf16[32,2048]{1,0:T(8,128)(2,1)} %bitcast.7, bf16[15,256,256]{2,1,0:T(8,128)(2,1)} %constant.10.clone.ramp_hbm, bf16[1024,1024]{1,0:T(8,128)(2,1)} %constant.11.clone.forward_hbm, ...), custom_call_target="tpu_custom_call" | custom-call | tf_op jit(solution)/shard_map/laminograph/pallas_call | solution.py:278
  24.2 0.0 copy-done
  24.2 1.3 %convolution_bitcast_fusion = f32[1,128,1024]{2,1,0:T(8,128)} fusion(bf16[1024,1024]{1,0:T(8,128)(2,1)S(1)} %copy-done, bf16[128,8,128]{2,1,0:T(8,128)(2,1)S(1)} %laminograph.1), kind=kOutput, calls=%fused_computation | convolution fusion | flops 268435456 | bytes 2883584 | tf_op jit(solution)/shard_map/dot_general | solution.py:311
Async XLA Ops:
  0.0 24.2 %copy-start = (bf16[1024,1024]{1,0:T(8,128)(2,1)S(1)}, bf16[1024,1024]{1,0:T(8,128)(2,1)}, u32[]{:S(2)}) copy-start(bf16[1024,1024]{1,0:T(8,128)(2,1)} %constant.12.clone) | copy-start | bytes 6291460

commit v8 on v7

--- a/solution.py
+++ b/solution.py
@@ -94,7 +94,7 @@
     angle_hbm, limit_hbm, trig_hbm, proj_hbm, ramp_hbm, forward_hbm, small_hbm,
     recv2,
     angle_ref, limit_ref, trig_ref, proj_ref, ramp_ref, forward_ref, small_ref,
-    stack_ref, filt_ref, g_ref, send1, recv1, rows_ref, gain_ref, back_ref, mix_ref, send2,
+    stack_ref, filt_ref, g_ref, send1, recv1, rows_ref, gain_ref, mix_ref, send2,
     limit_out, limit_in, table_sems, send_sems, recv_sems, limit_sems,
 ):
     d = lax.axis_index("depth")
@@ -251,13 +251,11 @@
     along_y = dot(small_ref[1], jnp.concatenate(tall, axis=1))
     back_y = dot(small_ref[2], (along_y * gain_ref[...]).astype(bf16)).astype(bf16)
     for k in range(KX):
-        back_ref[:, k * NY : (k + 1) * NY] = lax.dot_general(
+        mix_ref[:, k, :] = lax.dot_general(
             small_ref[0], back_y[:, k * NZ : (k + 1) * NZ], (((1,), (1,)), ((), ())), preferred_element_type=f32
         )
     for chunk in CHUNKS:
         first = pl.multiple_of(place2(chunk[0])[1][0] * BANDS, BANDS)
-        for k in range(KX):
-            mix_ref[pl.ds(first, BANDS), k, :] = back_ref[pl.ds(first, BANDS), k * NY : (k + 1) * NY]
         send2[pl.ds(first, BANDS)] = mix_ref[pl.ds(first, BANDS)].astype(bf16)
         for step in chunk:
             if any(step):
@@ -296,7 +294,6 @@
             pltpu.VMEM((N, 1, 2 * N), f32),
             pltpu.VMEM((3 * 256, YB * NZ), bf16),
             pltpu.VMEM((NZ, KX * NY), f32),
-            pltpu.VMEM((NZ, KX * NY), f32),
             pltpu.VMEM((NZ, KX, NY), f32),
             pltpu.VMEM((N, KX, NY), bf16),
             pltpu.VMEM((1, 1, N), f32),

time: 25.6 us -> 25.7 us (level)
  no operation moved by 1% of the time
where the time goes in v8:
time: 25.7 us; the launch traced here: 25.6 us
  Pallas kernels  24.4 us (95%)
  matrix products  1.27 us (5%)
    pallas_call x1, Pallas kernels, on_device(): pl.pallas_call(kernel, name='laminograph', out_shape=jax.ShapeDtypeStruct...  24.4 us
    dot_general x1, matrix products, on_device(): lax.dot_general(back.reshape(NX, NY), inverse, (((0,), (0,)), ((), ())),...  1.27 us

profile of v8, /device:TPU:1, one launch (start us, length us, event | category | flops | bytes accessed | tf_op | source)
XLA Modules:
  0.0 25.6 jit_solution(14880155268693833529)
XLA Ops:
  0.0 0.0 copy-start
  0.0 24.4 %laminograph.1 = bf16[128,8,128]{2,1,0:T(8,128)(2,1)S(1)} custom-call(s32[16]{0:T(128)} %angle_hbm.1, s32[1,2]{1,0:T(1,128)} %limit_hbm.1, f32[2880]{0:T(1024)} %constant.14.clone.trig_hbm, bf16[32,2048]{1,0:T(8,128)(2,1)} %bitcast.7, bf16[15,256,256]{2,1,0:T(8,128)(2,1)} %constant.10.clone.ramp_hbm, bf16[1024,1024]{1,0:T(8,128)(2,1)} %constant.11.clone.forward_hbm, ...), custom_call_target="tpu_custom_call" | custom-call | tf_op jit(solution)/shard_map/laminograph/pallas_call | solution.py:276
  24.4 0.0 copy-done
  24.4 1.3 %convolution_bitcast_fusion = f32[1,128,1024]{2,1,0:T(8,128)} fusion(bf16[1024,1024]{1,0:T(8,128)(2,1)S(1)} %copy-done, bf16[128,8,128]{2,1,0:T(8,128)(2,1)S(1)} %laminograph.1), kind=kOutput, calls=%fused_computation | convolution fusion | flops 268435456 | bytes 2883584 | tf_op jit(solution)/shard_map/dot_general | solution.py:308
Async XLA Ops:
  0.0 24.4 %copy-start = (bf16[1024,1024]{1,0:T(8,128)(2,1)S(1)}, bf16[1024,1024]{1,0:T(8,128)(2,1)}, u32[]{:S(2)}) copy-start(bf16[1024,1024]{1,0:T(8,128)(2,1)} %constant.12.clone) | copy-start | bytes 6291460
